TPU v7x, 128 devices: a whole 4x4x4 slice. The times are simulated.
128 devices in a mesh: ctx: 16 (over z, x_hi, core), shard: 8 (over y, x_lo).
Axes of the slice: x: 4 (x_hi: 2, x_lo: 2; x = x_hi * 2 + x_lo), y: 4, z: 4, core: 2. Of those that a mesh axis runs over, the one named last changes fastest.
Arguments:
- hidden: bfloat16 [16384, 2048], P('ctx'), may hold values from -6 to 6
- ids: int32 [16384], P('ctx'), may hold values from 0 to 4
- table: bfloat16 [5, 2048], replicated, may hold values from -3 to 3
- proj_weight: bfloat16 [2048, 2, 4096], P(None, None, 'shard'), may hold values from -0.125 to 0.125
- bc_weight: bfloat16 [2048, 256], P(None, 'shard'), may hold values from -0.01171875 to 0.01171875
- dt_weight: bfloat16 [2048, 64], P(None, 'shard'), may hold values from -0.125 to 0.125
- dt_bias: float32 [64], P('shard'), may hold values from -1 to 1
- decay: float32 [64], P('shard'), may hold values from 3.0517578e-05 to 0.04
- conv_weight: float32 [4, 4096], P(None, 'shard'), may hold values from -3 to 3
- conv_bias: float32 [4096], P('shard'), may hold values from -0.5 to 0.5
- skip: float32 [64], P('shard'), may hold values from 0.5 to 1.5
- norm_gain: float32 [4096], P('shard'), may hold values from 0.5 to 1.5
- out_weight: bfloat16 [4096, 2048], P('shard'), may hold values from -0.09375 to 0.09375
Outputs:
- mixed: bfloat16 [2048, 16384], P('shard', 'ctx')
All inputs are finite; a program needn't handle non-finite values.
Results may differ from a plain program's by a relative error of at most 0.0095.
Values may be sent and summed in bfloat16 or wider, within the bound.
A program may use at most 128 MiB of HBM per device.

v0:
```python
import jax
import jax.numpy as jnp
from jax import lax
from jax.experimental import pallas as pl
from jax.experimental.pallas import tpu as pltpu
from jax.sharding import PartitionSpec as P

E = 4096
L = 128
TB = 256
XR = 160
HEADDIM = 64
MESH = pl.DeviceIdType.MESH
F32 = jnp.float32
BF16 = jnp.bfloat16
NT = (((1,), (1,)), ((), ()))
TN = (((0,), (0,)), ((), ()))


def dot(a, b, dims=(((1,), (0,)), ((), ())), **kw):
    return lax.dot_general(a, b, dims, preferred_element_type=F32, **kw)


def silu(x):
    half = 0.5 * x
    return half + half * jnp.tanh(half)


def iota(shape, dim):
    return lax.broadcasted_iota(jnp.int32, shape, dim)


def split(x):
    hi = x.astype(BF16).astype(F32)
    return hi, (x - hi).astype(BF16).astype(F32)


def rows_of(k, size):
    return pl.ds(pl.multiple_of(k * size, size), size)


def kernel(
    hid_hbm, ids_ref, table_ref, wx_hbm, wg_hbm, bcw_hbm, dtw_ref, cw_ref, cb_ref, gain_ref, wo_hbm,
    dtb_ref, decay_ref, skip_ref,
    out_ref,
    u, ur, wx, wg, wall, bcw, flip, xin, xc, bc, gate, ybuf, eexp, dtraw, rowsbuf, cols, arow, sch, sst,
    halo_out, halo_in, st_out, st_in, ch_out, ch_in, pl_out, pl_in, fin_out, fin_in,
    sq, nrm, part, rx, qbuf, ry, ry2, abuf, rx2,
    hsem, wsem, bsem, bgs, bgr, bcs, bcr, hs, hr, sts, stsr, chs, chr_, pls, plr, fis, fir, sqs, sqr,
    rxs, rxr, rys, ryr, ry2s, ry2r, rx2s, rx2r,
):
    T, D = u.shape
    wexp = ybuf
    EL = xc.shape[2]
    NB = T // TB
    NC = T // L
    H = EL // HEADDIM
    c = lax.axis_index("ctx")
    s = lax.axis_index("shard")
    z, xh, core = c // 4, (c // 2) % 2, c % 2
    y, xl = s // 2, s % 2

    def remote(src, dst, ss, rs, ctx=None, shard=None):
        return pltpu.make_async_remote_copy(
            src_ref=src, dst_ref=dst, send_sem=ss, recv_sem=rs,
            device_id={"ctx": c if ctx is None else ctx, "shard": s if shard is None else shard},
            device_id_type=MESH,
        )

    hcopies = [
        pltpu.make_async_copy(hid_hbm.at[pl.ds(b * TB, TB)], u.at[pl.ds(b * TB, TB)], hsem.at[b])
        for b in range(NB)
    ]
    wxc = pltpu.make_async_copy(wx_hbm, wx, wsem.at[0])
    wgc = pltpu.make_async_copy(wg_hbm, wg, wsem.at[1])
    woc = pltpu.make_async_copy(wo_hbm, wall.at[pl.ds(0, EL)], wsem.at[2])
    bown = pltpu.make_async_copy(bcw_hbm.at[core], bcw.at[s, core], bsem)
    hcopies[0].start()
    wxc.start()
    bown.start()
    for b in range(1, NB):
        hcopies[b].start()
    wgc.start()
    woc.start()

    mate = c + 1 - 2 * core
    other = (c + 16 + 2 * core - 1) % 16
    xmate = c + 2 - 4 * xh
    barrier = pltpu.get_barrier_semaphore()
    peers = [(mate, s), (other, s), (xmate, s)]
    peers += [((c + 4 * k) % 16, s) for k in range(1, 4)]
    peers += [(c, (s + k) % 8) for k in range(1, 8)]
    for pc, ps in peers:
        pl.semaphore_signal(barrier, inc=1, device_id={"ctx": pc, "shard": ps}, device_id_type=MESH)
    pl.semaphore_wait(barrier, len(peers))

    def gather(k):
        return remote(bcw_hbm.at[core], bcw.at[s, core], bgs.at[k - 1], bgr.at[k - 1], shard=(s + k) % 8)

    for k in range(1, 8):
        gather(k).start()

    flip[...] = jnp.where(iota((TB, TB), 0) + iota((TB, TB), 1) == TB - 1, 1.0, 0.0).astype(BF16)
    wxc.wait()
    nd = D // TB

    def front(b, _):
        rows = rows_of(b, TB)
        pltpu.make_async_copy(hid_hbm.at[rows], u.at[rows], hsem.at[b]).wait()
        hot = jnp.where(iota((16, TB), 0) == ids_ref[:, rows], 1.0, 0.0).astype(BF16)
        added = dot(hot, table_ref[...], TN)
        u[rows, :] = (u[rows, :].astype(F32) + added).astype(BF16)
        for i in range(nd):
            ur[rows, i * TB:(i + 1) * TB] = dot(
                u[rows, (nd - 1 - i) * TB:(nd - i) * TB], flip[...]
            ).astype(BF16)
        for i, v in enumerate((u, ur)):
            xv = dot(v[rows, :], wx[...]).astype(BF16)
            xin[i, pl.ds(pl.multiple_of(b * TB + 8, 8), TB), :] = xv.astype(F32)
            dr = dot(dtw_ref[...], v[rows, :], NT)
            for q in range(TB // L):
                dtraw[i, rows_of(b * (TB // L) + q, H), :] = dr[:, q * L:(q + 1) * L]
        return 0

    lax.fori_loop(0, NB, front, 0)

    halo_out[0] = xin[0, T - 8:T + 8, :].astype(BF16)
    halo_out[1] = xin[1, 8:24, :].astype(BF16)
    nxt, prv = (c + 1) % 16, (c + 15) % 16
    hcf = remote(halo_out.at[0], halo_in.at[0], hs.at[0], hr.at[0], ctx=nxt)
    hcr = remote(halo_out.at[1], halo_in.at[1], hs.at[1], hr.at[1], ctx=prv)
    hcf.start()
    hcr.start()

    bown.wait()
    for k in range(1, 8):
        gather(k).wait()
    swap = remote(bcw.at[:, core], bcw.at[:, core], bcs, bcr, ctx=mate)
    swap.start()

    head = iota((NC * H, L), 0) % H
    bias = jnp.zeros((NC * H, L), F32)
    rate = jnp.zeros((NC * H, L), F32)
    for h in range(H):
        bias = jnp.where(head == h, dtb_ref[h], bias)
        rate = jnp.where(head == h, decay_ref[h], rate)
    rowsbuf[...] = jnp.zeros_like(rowsbuf)
    before = iota((L, L), 0) <= iota((L, L), 1)
    after = iota((L, L), 0) >= iota((L, L), 1)
    for i in range(2):
        raw = dtraw[i] + bias
        dt = jnp.maximum(raw, 0.0) + jnp.log1p(jnp.exp(-jnp.abs(raw)))
        tri = jnp.where(before if i == 0 else after, 1.0, 0.0)
        g = dot(-dt * rate, tri, precision=lax.Precision.HIGHEST)
        total = g[:, L - 1:L] if i == 0 else g[:, 0:1]
        whi, wlo = split(jnp.exp(total - g) * dt)
        ehi, elo = split(jnp.exp(g))
        a = g - jnp.log(dt)
        for k in range(NC):
            sl = slice(k * H, (k + 1) * H)
            arow[i, k] = a[sl]
            for j, part_ in enumerate((g, whi, wlo, ehi, elo)):
                at = (5 * i + j) * H
                rowsbuf[k, at:at + H, :] = part_[sl]

    er, ec = iota((L, EL), 0), iota((L, EL), 1)

    def spread(first):
        hit = (er >= first) & (er < first + 2 * H) & (er % H == ec // HEADDIM)
        return jnp.where(hit, 1.0, 0.0).astype(BF16)

    spreads = [spread(5 * H * i + H + 2 * H * j) for i in range(2) for j in range(2)]

    def expand(k, _):
        rows = rows_of(k, L)
        t = rowsbuf[k].T
        cols[rows, :] = t
        tb = t.astype(BF16)
        for i in range(2):
            wexp[i, rows, :] = dot(tb, spreads[2 * i])
            eexp[i, rows, :] = dot(tb, spreads[2 * i + 1])
        return 0

    lax.fori_loop(0, NC, expand, 0)

    swap.wait()

    def proj_bc(b, _):
        rows = rows_of(b, TB)
        wb = bcw[...].reshape(8 * 32, D)
        for i, v in enumerate((u, ur)):
            bc[i, rows, :] = dot(v[rows, :], wb, NT).astype(BF16)
        return 0

    lax.fori_loop(0, NB, proj_bc, 0)

    hcf.wait()
    hcr.wait()
    xin[0, 0:8, :] = jnp.where(c > 0, halo_in[0, 8:16, :].astype(F32), 0.0)
    xin[1, T + 8:T + 16, :] = jnp.where(c < 15, halo_in[1, 0:8, :].astype(F32), 0.0)

    def chunk_state(k, _):
        rows = rows_of(k, L)
        for i in range(2):
            window = xin[i, pl.ds(pl.multiple_of(k * L, L), L + 16), :]
            acc = jnp.zeros((L, EL), F32) + cb_ref[...]
            for t in range(4):
                at = 8 - 3 + t if i == 0 else 8 + 3 - t
                acc = acc + cw_ref[t:t + 1, :] * window[at:at + L, :]
            xv = silu(acc).astype(BF16)
            xc[i, rows, :] = xv
            scaled = (wexp[i, rows, :] * xv.astype(F32)).astype(BF16)
            bt = bc[i, rows, 0:L].astype(F32).T.astype(BF16)
            sch[i, k] = dot(bt, scaled)
        return 0

    lax.fori_loop(0, NC, chunk_state, 0)

    def chunk_decay(i, k):
        at = k * L + (L - 1 if i == 0 else 0)
        return eexp[i, at:at + 1, :]

    def pack_decay(d):
        hi, lo = split(d)
        wide = (8, d.shape[1])
        return jnp.concatenate([jnp.broadcast_to(hi, wide), jnp.broadcast_to(lo, wide)], 0).astype(BF16)

    def load_state(ref):
        whole = ref[...]
        tail = whole[L:L + 16].astype(F32)
        return whole[:L].astype(F32), tail[0:1] + tail[8:9]

    for i in range(2):
        state, dec = None, None
        for k in (range(NC) if i == 0 else range(NC - 1, -1, -1)):
            d = chunk_decay(i, k)
            state = sch[i, k] if state is None else d * state + sch[i, k]
            dec = d if dec is None else dec * d
        st_out[i, 0:L, :] = state.astype(BF16)
        st_out[i, L:L + 16, :] = pack_decay(dec)

    sta = remote(st_out, st_in, sts, stsr, ctx=mate)
    sta.start()

    wgc.wait()

    def proj_gate(b, _):
        rows = rows_of(b, TB)
        for i, v in enumerate((u, ur)):
            gate[i, rows, :] = silu(dot(v[rows, :], wg[...]))
        return 0

    lax.fori_loop(0, NB // 2, proj_gate, 0)

    sta.wait()
    HC = EL // 2
    half = pl.ds(pl.multiple_of(core * HC, HC), HC)
    for i in range(2):
        ms, md = load_state(st_out.at[i, :, half])
        ts, td = load_state(st_in.at[i, :, half])
        mine_first = core == i
        state = jnp.where(mine_first, td * ms + ts, md * ts + ms)
        ch_out[i, 0:L, :] = state.astype(BF16)
        ch_out[i, L:L + 16, :] = pack_decay(md * td)
    cha = remote(ch_out, ch_in, chs, chr_, ctx=xmate)
    cha.start()

    lax.fori_loop(NB // 2, NB, proj_gate, 0)

    woc.wait()
    for i in range(nd):
        wall[EL:2 * EL, i * TB:(i + 1) * TB] = dot(
            wall[0:EL, (nd - 1 - i) * TB:(nd - i) * TB], flip[...]
        ).astype(BF16)

    cha.wait()
    for i in range(2):
        ms, md = load_state(ch_out.at[i])
        ts, td = load_state(ch_in.at[i])
        mine_first = xh == i
        state = jnp.where(mine_first, td * ms + ts, md * ts + ms)
        pl_out[i, 0:L, :] = state.astype(BF16)
        pl_out[i, L:L + 16, :] = pack_decay(md * td)

    def plane(k):
        return remote(
            pl_out.at[(z + k) // 4], pl_in.at[z], pls.at[k - 1], plr.at[k - 1], ctx=(c + 4 * k) % 16
        )

    for k in range(1, 4):
        plane(k).start()
    pl_in[z] = pl_out[0]

    lane = iota((L, L), 1)
    sk = jnp.zeros((1, EL), F32)
    for h in range(H):
        sk = jnp.where(iota((1, EL), 1) // HEADDIM == h, skip_ref[h], sk)

    def intra(k, _):
        rows = rows_of(k, L)
        for i in range(2):
            cb = dot(bc[i, rows, L:2 * L], bc[i, rows, 0:L], NT)
            keep = iota((L, L), 0) >= lane if i == 0 else iota((L, L), 0) <= lane
            ar = arow[i, k]
            for q in range(H // 2):
                ms = []
                for h in (2 * q, 2 * q + 1):
                    at = 5 * H * i + h
                    d = cols[rows, at:at + 1] - ar[h:h + 1, :]
                    ms.append((jnp.exp(jnp.where(keep, d, -1e30)) * cb).astype(BF16))
                xp = xc[i, rows, q * L:(q + 1) * L]
                zero = jnp.zeros_like(xp)
                left = jnp.where(lane < HEADDIM, xp, zero)
                right = jnp.where(lane < HEADDIM, zero, xp)
                yq = dot(jnp.concatenate(ms, 1), jnp.concatenate([left, right], 0))
                ybuf[i, rows, q * L:(q + 1) * L] = yq + sk[:, q * L:(q + 1) * L] * xp.astype(F32)
        return 0

    lax.fori_loop(0, NC, intra, 0)

    for k in range(1, 4):
        plane(k).wait_send()
        pltpu.make_async_remote_copy(
            src_ref=pl_out.at[0], dst_ref=pl_in.at[(z + 4 - k) % 4], send_sem=pls.at[k - 1],
            recv_sem=plr.at[k - 1], device_id={"ctx": (c + 4 * k) % 16, "shard": s}, device_id_type=MESH,
        ).wait_recv()
    for i in range(2):
        acc = jnp.zeros((L, HC), F32)
        for zz in (range(3) if i == 0 else range(3, 0, -1)):
            ps, pd = load_state(pl_in.at[zz])
            acc = jnp.where((zz < z) if i == 0 else (zz > z), pd * acc + ps, acc)
        ts, td = load_state(ch_in.at[i])
        acc = jnp.where(xh != i, td * acc + ts, acc)
        fin_out[i] = acc.astype(BF16)
    fina = remote(fin_out, fin_in, fis, fir, ctx=mate)
    fina.start()
    fina.wait()

    for i in range(2):
        mine, theirs = fin_out[i].astype(F32), fin_in[i].astype(F32)
        entering = jnp.where(
            core == 0, jnp.concatenate([mine, theirs], 1), jnp.concatenate([theirs, mine], 1)
        )
        ts, td = load_state(st_in.at[i])
        state = jnp.where(core != i, td * entering + ts, entering)
        order = range(NC) if i == 0 else range(NC - 1, -1, -1)
        for k in order:
            sst[i, k] = state.astype(BF16)
            state = chunk_decay(i, k) * state + sch[i, k]

    def sums(j, k):
        return remote(sq.at[j, s], sq.at[j, s], sqs.at[j, k - 1], sqr.at[j, k - 1], shard=(s + k) % 8)

    def gated_block(j):
        total = jnp.zeros((8, TB), F32)
        for i in range(2):
            pick = jnp.where(iota((8, EL), 0) // 4 == i, 1.0, 0.0).astype(BF16)
            for q in range(TB // L):
                k = j * (TB // L) + q
                rows = slice(k * L, (k + 1) * L)
                yv = ybuf[i, rows, :] + eexp[i, rows, :] * dot(bc[i, rows, L:2 * L], sst[i, k])
                ybuf[i, rows, :] = yv * gate[i, rows, :]
            rows = slice(j * TB, (j + 1) * TB)
            gv = ybuf[i, rows, :]
            total = total + dot(pick, (gv * gv).astype(BF16), NT)
        sq[j, s] = total
        for k in range(1, 8):
            sums(j, k).start()

    def wait_sums(j):
        for k in range(1, 8):
            sums(j, k).wait_send()
            pltpu.make_async_remote_copy(
                src_ref=sq.at[j, s], dst_ref=sq.at[j, (s + 8 - k) % 8], send_sem=sqs.at[j, k - 1],
                recv_sem=sqr.at[j, k - 1], device_id={"ctx": c, "shard": (s + k) % 8}, device_id_type=MESH,
            ).wait_recv()

    xs = s + 1 - 2 * xl

    def cross(j):
        return remote(
            part.at[j, 1 - xl, :, pl.ds(0, XR), :], rx.at[j], rxs.at[j], rxr.at[j], shard=xs
        )

    def along(j, k):
        yk = (y + k) % 4
        return remote(
            part.at[j, :, yk, pl.ds(XR, TB - XR), :], ry2.at[j, k - 1], ry2s.at[j, k - 1], ry2r.at[j, k - 1],
            shard=yk * 2 + xl,
        )

    def along2(j, k):
        yk = (y + k) % 4
        return remote(qbuf.at[j, yk], ry.at[j, k - 1], rys.at[j, k - 1], ryr.at[j, k - 1], shard=yk * 2 + xl)

    def cross2(j):
        return remote(abuf.at[j], rx2.at[j], rx2s.at[j], rx2r.at[j], shard=xs)

    def product_block(j):
        wait_sums(j)
        total = sq[j, 0]
        for k in range(1, 8):
            total = total + sq[j, k]
        scale = lax.rsqrt(total / E + 1e-05)
        rows = slice(j * TB, (j + 1) * TB)
        for q in range(TB // L):
            col = jnp.concatenate([scale[:, q * L:(q + 1) * L]] * (L // 8), 0).T
            sub = slice(j * TB + q * L, j * TB + (q + 1) * L)
            for i in range(2):
                nv = ybuf[i, sub, :] * col[:, 4 * i:4 * i + 1] * gain_ref[...]
                nrm[sub, i * EL:(i + 1) * EL] = nv.astype(BF16)

        def piece(p, _):
            xx = lax.rem(p // 4 + 1 + xl, 2)
            yy = lax.rem(p, 4)
            colsl = rows_of(yy * 2 + xx, TB)
            part[j, xx, yy] = dot(nrm[rows, :], wall[:, colsl]).astype(BF16)
            return 0

        lax.fori_loop(0, 4, piece, 0)
        cross(j).start()
        lax.fori_loop(4, 8, piece, 0)
        for k in range(1, 4):
            along(j, k).start()

    def middle_block(j):
        cross(j).wait()
        for k in range(4):
            yk = (y + k) % 4
            both = part[j, xl, yk, 0:XR, :].astype(F32) + rx[j, yk].astype(F32)
            qbuf[j, yk] = both.astype(BF16)
            if k:
                along2(j, k).start()
        for k in range(1, 4):
            along(j, k).wait()
        for m in range(2):
            xx = (xl + 1 + m) % 2
            acc = part[j, xx, y, XR:TB, :].astype(F32)
            for k in range(1, 4):
                acc = acc + ry2[j, k - 1, xx].astype(F32)
            if m == 0:
                abuf[j] = acc.astype(BF16)
                cross2(j).start()
            else:
                keepbuf = acc
        return keepbuf

    def last_block(j, own):
        for k in range(1, 4):
            along2(j, k).wait()
        acc = qbuf[j, y].astype(F32)
        for k in range(1, 4):
            acc = acc + ry[j, k - 1].astype(F32)
        cross2(j).wait()
        low = own + rx2[j].astype(F32)
        whole = jnp.concatenate([acc, low], 0)
        out_ref[:, j * TB:(j + 1) * TB] = whole.T.astype(BF16)

    kept = [None] * NB
    gated_block(0)
    gated_block(1)
    product_block(0)
    gated_block(2)
    product_block(1)
    gated_block(3)
    kept[0] = middle_block(0)
    product_block(2)
    kept[1] = middle_block(1)
    product_block(3)
    kept[2] = middle_block(2)
    kept[3] = middle_block(3)
    for j in range(NB):
        last_block(j, kept[j])


def per_device(
    hidden, ids, table, proj_weight, bc_weight, dt_weight, dt_bias, decay, conv_weight, conv_bias, skip,
    norm_gain, out_weight,
):
    T, D = hidden.shape
    EL = conv_bias.shape[0]
    H = EL // HEADDIM
    NB, NC = T // TB, T // L
    vm = pl.BlockSpec(memory_space=pltpu.VMEM)
    sm = pl.BlockSpec(memory_space=pltpu.SMEM)
    hbm = pl.BlockSpec(memory_space=pl.ANY)
    V = pltpu.VMEM
    dma = pltpu.SemaphoreType.DMA
    scratch = [
        V((T, D), BF16), V((T, D), BF16),
        V((D, EL), BF16), V((D, EL), BF16), V((2 * EL, D), BF16),
        V((8, 2, 16, D), BF16), V((TB, TB), BF16),
        V((2, T + 16, EL), F32), V((2, T, EL), BF16), V((2, T, 2 * L), BF16),
        V((2, T, EL), F32), V((2, T, EL), F32), V((2, T, EL), F32),
        V((2, NC * H, L), F32), V((NC, L, L), F32), V((T, L), F32), V((2, NC, H, L), F32),
        V((2, NC, L, EL), F32), V((2, NC, L, EL), BF16),
        V((2, 16, EL), BF16), V((2, 16, EL), BF16),
        V((2, L + 16, EL), BF16), V((2, L + 16, EL), BF16),
        V((2, L + 16, EL // 2), BF16), V((2, L + 16, EL // 2), BF16),
        V((2, L + 16, EL // 2), BF16), V((4, L + 16, EL // 2), BF16),
        V((2, L, EL // 2), BF16), V((2, L, EL // 2), BF16),
        V((NB, 8, 8, TB), F32), V((T, 2 * EL), BF16), V((NB, 2, 4, TB, TB), BF16),
        V((NB, 4, XR, TB), BF16), V((NB, 4, XR, TB), BF16), V((NB, 3, XR, TB), BF16),
        V((NB, 3, 2, TB - XR, TB), BF16), V((NB, TB - XR, TB), BF16), V((NB, TB - XR, TB), BF16),
        dma((NB,)), dma((3,)), dma, dma((7,)), dma((7,)), dma, dma, dma((2,)), dma((2,)), dma, dma, dma, dma,
        dma((3,)), dma((3,)), dma, dma, dma((NB, 7)), dma((NB, 7)),
        dma((NB,)), dma((NB,)), dma((NB, 3)), dma((NB, 3)), dma((NB, 3)), dma((NB, 3)), dma((NB,)), dma((NB,)),
    ]
    return pl.pallas_call(
        kernel,
        out_shape=jax.ShapeDtypeStruct((D // 8, T), BF16),
        in_specs=[hbm, vm, vm, hbm, hbm, hbm, vm, vm, vm, vm, hbm, sm, sm, sm],
        out_specs=vm,
        scratch_shapes=scratch,
        compiler_params=pltpu.CompilerParams(
            collective_id=0, has_side_effects=True, vmem_limit_bytes=60 * 1024 * 1024
        ),
        cost_estimate=pl.CostEstimate(flops=20_000_000_000, bytes_accessed=16_000_000, transcendentals=4_000_000),
    )(
        hidden, ids.reshape(1, T), jnp.pad(table, ((0, 16 - table.shape[0]), (0, 0))),
        proj_weight[:, 1, :], proj_weight[:, 0, :], bc_weight.T.reshape(2, 16, D), dt_weight.T,
        conv_weight, conv_bias.reshape(1, EL), norm_gain.reshape(1, EL), out_weight,
        dt_bias, decay, skip,
    )


def solution(mesh):
    in_specs = (
        P("ctx", None), P("ctx"), P(), P(None, None, "shard"), P(None, "shard"), P(None, "shard"), P("shard"),
        P("shard"), P(None, "shard"), P("shard"), P("shard"), P("shard"), P("shard", None),
    )
    return jax.shard_map(
        per_device, mesh=mesh, in_specs=in_specs, out_specs=P("shard", "ctx"), check_vma=False
    )
```

profile of v0, /device:TPU:0, one launch (start us, length us, event | category | flops | bytes accessed | tf_op | source)
XLA Modules:
  0.0 106.5 jit_solution(4778065797421673016)
XLA Ops:
  0.0 8.9 %fusion = (bf16[2048,1,512]{2,1,0:T(2,128)(2,1)S(1)}, bf16[2048,1,512]{2,1,0:T(2,128)(2,1)S(1)}) fusion(bf16[2048,2,512]{2,1,0:T(2,128)(2,1)} %param.16), kind=kLoop, calls=%fused_computation.2 | loop fusion | bytes 8388608 | tf_op jit(solution)/shard_map/slice | solution.py:521
  9.0 0.0 copy-start
  9.0 3.2 %copy_bitcast_fusion = (bf16[2048,512]{1,0:T(8,128)(2,1)}, bf16[2048,512]{1,0:T(8,128)(2,1)}) fusion(bf16[2048,1,512]{2,1,0:T(2,128)(2,1)S(1)} %get-tuple-element.5, bf16[2048,1,512]{2,1,0:T(2,128)(2,1)S(1)} %get-tuple-element.6), kind=kLoop, calls=%fused_computation | loop fusion | bytes 8388608 | tf_op jit(solution)/shard_map/squeeze | solution.py:521
  12.1 0.0 copy-done
  12.1 0.6 pad.4.table_ref
  12.8 91.9 %shard_map.127 = bf16[256,1024]{1,0:T(8,128)(2,1)} custom-call(bf16[1024,2048]{1,0:T(8,128)(2,1)} %hid_hbm.1, s32[1,1024]{1,0:T(1,128)} %bitcast.13, bf16[16,2048]{1,0:T(8,128)(2,1)} %pad.4.table_ref, bf16[2048,512]{1,0:T(8,128)(2,1)} %get-tuple-element.8.wx_hbm, bf16[2048,512]{1,0:T(8,128)(2,1)} %get-tuple-element.7.wg_hbm, bf16[2,16,2048]{2,1,0:T(8,128)(2,1)} %bitcast.11, ...), custom_call_target="tpu_custom_call" | custom-call | flops 20000000000 | bytes 16000000 | tf_op jit(solution)/shard_map/pallas_call | solution.py:509
  104.6 1.9 %copy.21 = bf16[256,1024]{1,0:T(8,128)(2,1)} copy(bf16[256,1024]{1,0:T(8,128)(2,1)} %shard_map.127) | data formatting | bytes 1048576
Async XLA Ops:
  9.0 3.2 %copy-start = (bf16[5,2048]{1,0:T(8,128)(2,1)S(1)}, bf16[5,2048]{1,0:T(8,128)(2,1)}, u32[]{:S(2)}) copy-start(bf16[5,2048]{1,0:T(8,128)(2,1)} %param.15) | copy-start | bytes 61444
where the time goes:
time: 107 us
  Pallas kernels  91.9 us (86%)
  local copies, waits for them, and re-layouts  14.6 us (14%)
    pallas_call x1, Pallas kernels, per_device(): pl.pallas_call(kernel, out_shape=jax.ShapeDtypeStruct((D // 8, T), BF16),...  91.9 us
    slice x1, local copies, waits for them, and re-layouts, per_device(): proj_weight[:, 0, :]  8.94 us
    squeeze x1, local copies, waits for them, and re-layouts, per_device(): proj_weight[:, 0, :]  3.17 us

commit v1 on v0

--- a/solution.py
+++ b/solution.py
@@ -40,17 +40,16 @@
 
 
 def kernel(
-    hid_hbm, ids_ref, table_ref, wx_hbm, wg_hbm, bcw_hbm, dtw_ref, cw_ref, cb_ref, gain_ref, wo_hbm,
+    hid_hbm, ids_ref, table_ref, w_hbm, bcw_hbm, dtw_ref, cw_ref, cb_ref, gain_ref, wo_hbm,
     dtb_ref, decay_ref, skip_ref,
     out_ref,
-    u, ur, wx, wg, wall, bcw, flip, xin, xc, bc, gate, ybuf, eexp, dtraw, rowsbuf, cols, arow, sch, sst,
+    u, ur, wraw, wx, wg, wall, bcw, flip, xin, xc, bc, gate, ybuf, dtraw, rowsbuf, cols, arow, sch, sst,
     halo_out, halo_in, st_out, st_in, ch_out, ch_in, pl_out, pl_in, fin_out, fin_in,
     sq, nrm, part, rx, qbuf, ry, ry2, abuf, rx2,
-    hsem, wsem, bsem, bgs, bgr, bcs, bcr, hs, hr, sts, stsr, chs, chr_, pls, plr, fis, fir, sqs, sqr,
+    hsem, wsem, wosem, bsem, bgs, bgr, bcs, bcr, hs, hr, sts, stsr, chs, chr_, pls, plr, fis, fir, sqs, sqr,
     rxs, rxr, rys, ryr, ry2s, ry2r, rx2s, rx2r,
 ):
     T, D = u.shape
-    wexp = ybuf
     EL = xc.shape[2]
     NB = T // TB
     NC = T // L
@@ -67,21 +66,21 @@
             device_id_type=MESH,
         )
 
+    WR = D // NB
     hcopies = [
         pltpu.make_async_copy(hid_hbm.at[pl.ds(b * TB, TB)], u.at[pl.ds(b * TB, TB)], hsem.at[b])
         for b in range(NB)
     ]
-    wxc = pltpu.make_async_copy(wx_hbm, wx, wsem.at[0])
-    wgc = pltpu.make_async_copy(wg_hbm, wg, wsem.at[1])
-    woc = pltpu.make_async_copy(wo_hbm, wall.at[pl.ds(0, EL)], wsem.at[2])
+    wcopies = [
+        pltpu.make_async_copy(w_hbm.at[pl.ds(b * WR, WR)], wraw.at[pl.ds(b * WR, WR)], wsem.at[b])
+        for b in range(NB)
+    ]
+    woc = pltpu.make_async_copy(wo_hbm, wall.at[pl.ds(0, EL)], wosem)
     bown = pltpu.make_async_copy(bcw_hbm.at[core], bcw.at[s, core], bsem)
-    hcopies[0].start()
-    wxc.start()
+    for b in range(NB):
+        hcopies[b].start()
+        wcopies[b].start()
     bown.start()
-    for b in range(1, NB):
-        hcopies[b].start()
-    wgc.start()
-    woc.start()
 
     mate = c + 1 - 2 * core
     other = (c + 16 + 2 * core - 1) % 16
@@ -101,28 +100,35 @@
         gather(k).start()
 
     flip[...] = jnp.where(iota((TB, TB), 0) + iota((TB, TB), 1) == TB - 1, 1.0, 0.0).astype(BF16)
-    wxc.wait()
     nd = D // TB
-
-    def front(b, _):
-        rows = rows_of(b, TB)
-        pltpu.make_async_copy(hid_hbm.at[rows], u.at[rows], hsem.at[b]).wait()
-        hot = jnp.where(iota((16, TB), 0) == ids_ref[:, rows], 1.0, 0.0).astype(BF16)
+    for b in range(NB):
+        rows = slice(b * TB, (b + 1) * TB)
+        hcopies[b].wait()
+        hot = jnp.where(iota((table_ref.shape[0], TB), 0) == ids_ref[:, rows], 1.0, 0.0).astype(BF16)
         added = dot(hot, table_ref[...], TN)
         u[rows, :] = (u[rows, :].astype(F32) + added).astype(BF16)
         for i in range(nd):
             ur[rows, i * TB:(i + 1) * TB] = dot(
                 u[rows, (nd - 1 - i) * TB:(nd - i) * TB], flip[...]
             ).astype(BF16)
+        wcopies[b].wait()
+        for k in range(WR // L):
+            wr = slice(b * WR + k * L, b * WR + (k + 1) * L)
+            pair = jnp.swapaxes(wraw[wr, :, :], 0, 1)
+            wg[wr, :] = pair[0]
+            wx[wr, :] = pair[1]
+    woc.start()
+
+    PB = 512
+    for b in range(T // PB):
+        rows = slice(b * PB, (b + 1) * PB)
         for i, v in enumerate((u, ur)):
             xv = dot(v[rows, :], wx[...]).astype(BF16)
-            xin[i, pl.ds(pl.multiple_of(b * TB + 8, 8), TB), :] = xv.astype(F32)
+            xin[i, 8 + b * PB:8 + (b + 1) * PB, :] = xv.astype(F32)
             dr = dot(dtw_ref[...], v[rows, :], NT)
-            for q in range(TB // L):
-                dtraw[i, rows_of(b * (TB // L) + q, H), :] = dr[:, q * L:(q + 1) * L]
-        return 0
-
-    lax.fori_loop(0, NB, front, 0)
+            for q in range(PB // L):
+                k = b * (PB // L) + q
+                dtraw[i, k * H:(k + 1) * H, :] = dr[:, q * L:(q + 1) * L]
 
     halo_out[0] = xin[0, T - 8:T + 8, :].astype(BF16)
     halo_out[1] = xin[1, 8:24, :].astype(BF16)
@@ -147,6 +153,7 @@
     rowsbuf[...] = jnp.zeros_like(rowsbuf)
     before = iota((L, L), 0) <= iota((L, L), 1)
     after = iota((L, L), 0) >= iota((L, L), 1)
+    decs = []
     for i in range(2):
         raw = dtraw[i] + bias
         dt = jnp.maximum(raw, 0.0) + jnp.log1p(jnp.exp(-jnp.abs(raw)))
@@ -156,6 +163,11 @@
         whi, wlo = split(jnp.exp(total - g) * dt)
         ehi, elo = split(jnp.exp(g))
         a = g - jnp.log(dt)
+        owner = iota((NC * H, EL), 0) % H == iota((NC * H, EL), 1) // HEADDIM
+        chunk_of = jnp.where(iota((NC, NC * H), 1) // H == iota((NC, NC * H), 0), 1.0, 0.0).astype(BF16)
+        thi, tlo = split(jnp.where(owner, jnp.exp(total), 0.0))
+        dec_rows = dot(chunk_of, thi.astype(BF16)) + dot(chunk_of, tlo.astype(BF16))
+        decs.append([dec_rows[k:k + 1, :] for k in range(NC)])
         for k in range(NC):
             sl = slice(k * H, (k + 1) * H)
             arow[i, k] = a[sl]
@@ -170,29 +182,14 @@
         return jnp.where(hit, 1.0, 0.0).astype(BF16)
 
     spreads = [spread(5 * H * i + H + 2 * H * j) for i in range(2) for j in range(2)]
-
-    def expand(k, _):
-        rows = rows_of(k, L)
-        t = rowsbuf[k].T
-        cols[rows, :] = t
-        tb = t.astype(BF16)
-        for i in range(2):
-            wexp[i, rows, :] = dot(tb, spreads[2 * i])
-            eexp[i, rows, :] = dot(tb, spreads[2 * i + 1])
-        return 0
-
-    lax.fori_loop(0, NC, expand, 0)
+    for k in range(NC):
+        cols[k * L:(k + 1) * L, :] = rowsbuf[k].T
 
     swap.wait()
-
-    def proj_bc(b, _):
-        rows = rows_of(b, TB)
-        wb = bcw[...].reshape(8 * 32, D)
+    for b in range(T // PB):
+        rows = slice(b * PB, (b + 1) * PB)
         for i, v in enumerate((u, ur)):
-            bc[i, rows, :] = dot(v[rows, :], wb, NT).astype(BF16)
-        return 0
-
-    lax.fori_loop(0, NB, proj_bc, 0)
+            bc[i, rows, :] = dot(v[rows, :], bcw[...].reshape(8 * 32, D), NT).astype(BF16)
 
     hcf.wait()
     hcr.wait()
@@ -209,16 +206,13 @@
                 acc = acc + cw_ref[t:t + 1, :] * window[at:at + L, :]
             xv = silu(acc).astype(BF16)
             xc[i, rows, :] = xv
-            scaled = (wexp[i, rows, :] * xv.astype(F32)).astype(BF16)
+            wexp = dot(cols[rows, :].astype(BF16), spreads[2 * i])
+            scaled = (wexp * xv.astype(F32)).astype(BF16)
             bt = bc[i, rows, 0:L].astype(F32).T.astype(BF16)
             sch[i, k] = dot(bt, scaled)
         return 0
 
-    lax.fori_loop(0, NC, chunk_state, 0)
-
-    def chunk_decay(i, k):
-        at = k * L + (L - 1 if i == 0 else 0)
-        return eexp[i, at:at + 1, :]
+    lax.fori_loop(0, NC, chunk_state, 0, unroll=2)
 
     def pack_decay(d):
         hi, lo = split(d)
@@ -233,7 +227,7 @@
     for i in range(2):
         state, dec = None, None
         for k in (range(NC) if i == 0 else range(NC - 1, -1, -1)):
-            d = chunk_decay(i, k)
+            d = decs[i][k]
             state = sch[i, k] if state is None else d * state + sch[i, k]
             dec = d if dec is None else dec * d
         st_out[i, 0:L, :] = state.astype(BF16)
@@ -242,15 +236,39 @@
     sta = remote(st_out, st_in, sts, stsr, ctx=mate)
     sta.start()
 
-    wgc.wait()
-
-    def proj_gate(b, _):
-        rows = rows_of(b, TB)
+    lane = iota((L, L), 1)
+    sk = jnp.zeros((1, EL), F32)
+    for h in range(H):
+        sk = jnp.where(iota((1, EL), 1) // HEADDIM == h, skip_ref[h], sk)
+
+    def late_block(j):
+        rows = slice(j * TB, (j + 1) * TB)
         for i, v in enumerate((u, ur)):
             gate[i, rows, :] = silu(dot(v[rows, :], wg[...]))
-        return 0
-
-    lax.fori_loop(0, NB // 2, proj_gate, 0)
+        for k in range(j * (TB // L), (j + 1) * (TB // L)):
+            rows = slice(k * L, (k + 1) * L)
+            for i in range(2):
+                cb = dot(bc[i, rows, L:2 * L], bc[i, rows, 0:L], NT)
+                keep = iota((L, L), 0) >= lane if i == 0 else iota((L, L), 0) <= lane
+                ar = arow[i, k]
+                for q in range(H // 2):
+                    ms = []
+                    for h in (2 * q, 2 * q + 1):
+                        at = 5 * H * i + h
+                        d = cols[rows, at:at + 1] - ar[h:h + 1, :]
+                        ms.append((jnp.exp(jnp.where(keep, d, -1e30)) * cb).astype(BF16))
+                    xp = xc[i, rows, q * L:(q + 1) * L]
+                    zero = jnp.zeros_like(xp)
+                    left = jnp.where(lane < HEADDIM, xp, zero)
+                    right = jnp.where(lane < HEADDIM, zero, xp)
+                    yq = dot(jnp.concatenate(ms, 1), jnp.concatenate([left, right], 0))
+                    ybuf[i, rows, q * L:(q + 1) * L] = yq + sk[:, q * L:(q + 1) * L] * xp.astype(F32)
+
+    woc.wait()
+    for i in range(nd):
+        wall[EL:2 * EL, i * TB:(i + 1) * TB] = dot(
+            wall[0:EL, (nd - 1 - i) * TB:(nd - i) * TB], flip[...]
+        ).astype(BF16)
 
     sta.wait()
     HC = EL // 2
@@ -265,13 +283,7 @@
     cha = remote(ch_out, ch_in, chs, chr_, ctx=xmate)
     cha.start()
 
-    lax.fori_loop(NB // 2, NB, proj_gate, 0)
-
-    woc.wait()
-    for i in range(nd):
-        wall[EL:2 * EL, i * TB:(i + 1) * TB] = dot(
-            wall[0:EL, (nd - 1 - i) * TB:(nd - i) * TB], flip[...]
-        ).astype(BF16)
+    late_block(0)
 
     cha.wait()
     for i in range(2):
@@ -291,32 +303,7 @@
         plane(k).start()
     pl_in[z] = pl_out[0]
 
-    lane = iota((L, L), 1)
-    sk = jnp.zeros((1, EL), F32)
-    for h in range(H):
-        sk = jnp.where(iota((1, EL), 1) // HEADDIM == h, skip_ref[h], sk)
-
-    def intra(k, _):
-        rows = rows_of(k, L)
-        for i in range(2):
-            cb = dot(bc[i, rows, L:2 * L], bc[i, rows, 0:L], NT)
-            keep = iota((L, L), 0) >= lane if i == 0 else iota((L, L), 0) <= lane
-            ar = arow[i, k]
-            for q in range(H // 2):
-                ms = []
-                for h in (2 * q, 2 * q + 1):
-                    at = 5 * H * i + h
-                    d = cols[rows, at:at + 1] - ar[h:h + 1, :]
-                    ms.append((jnp.exp(jnp.where(keep, d, -1e30)) * cb).astype(BF16))
-                xp = xc[i, rows, q * L:(q + 1) * L]
-                zero = jnp.zeros_like(xp)
-                left = jnp.where(lane < HEADDIM, xp, zero)
-                right = jnp.where(lane < HEADDIM, zero, xp)
-                yq = dot(jnp.concatenate(ms, 1), jnp.concatenate([left, right], 0))
-                ybuf[i, rows, q * L:(q + 1) * L] = yq + sk[:, q * L:(q + 1) * L] * xp.astype(F32)
-        return 0
-
-    lax.fori_loop(0, NC, intra, 0)
+    late_block(1)
 
     for k in range(1, 4):
         plane(k).wait_send()
@@ -346,7 +333,7 @@
         order = range(NC) if i == 0 else range(NC - 1, -1, -1)
         for k in order:
             sst[i, k] = state.astype(BF16)
-            state = chunk_decay(i, k) * state + sch[i, k]
+            state = decs[i][k] * state + sch[i, k]
 
     def sums(j, k):
         return remote(sq.at[j, s], sq.at[j, s], sqs.at[j, k - 1], sqr.at[j, k - 1], shard=(s + k) % 8)
@@ -358,7 +345,8 @@
             for q in range(TB // L):
                 k = j * (TB // L) + q
                 rows = slice(k * L, (k + 1) * L)
-                yv = ybuf[i, rows, :] + eexp[i, rows, :] * dot(bc[i, rows, L:2 * L], sst[i, k])
+                eexp = dot(cols[rows, :].astype(BF16), spreads[2 * i + 1])
+                yv = ybuf[i, rows, :] + eexp * dot(bc[i, rows, L:2 * L], sst[i, k])
                 ybuf[i, rows, :] = yv * gate[i, rows, :]
             rows = slice(j * TB, (j + 1) * TB)
             gv = ybuf[i, rows, :]
@@ -410,16 +398,12 @@
                 nv = ybuf[i, sub, :] * col[:, 4 * i:4 * i + 1] * gain_ref[...]
                 nrm[sub, i * EL:(i + 1) * EL] = nv.astype(BF16)
 
-        def piece(p, _):
+        for p in range(8):
             xx = lax.rem(p // 4 + 1 + xl, 2)
-            yy = lax.rem(p, 4)
-            colsl = rows_of(yy * 2 + xx, TB)
-            part[j, xx, yy] = dot(nrm[rows, :], wall[:, colsl]).astype(BF16)
-            return 0
-
-        lax.fori_loop(0, 4, piece, 0)
-        cross(j).start()
-        lax.fori_loop(4, 8, piece, 0)
+            yy = p % 4
+            part[j, xx, yy] = dot(nrm[rows, :], wall[:, rows_of(yy * 2 + xx, TB)]).astype(BF16)
+            if p == 3:
+                cross(j).start()
         for k in range(1, 4):
             along(j, k).start()
 
@@ -460,8 +444,10 @@
     gated_block(0)
     gated_block(1)
     product_block(0)
+    late_block(2)
     gated_block(2)
     product_block(1)
+    late_block(3)
     gated_block(3)
     kept[0] = middle_block(0)
     product_block(2)
@@ -488,10 +474,10 @@
     dma = pltpu.SemaphoreType.DMA
     scratch = [
         V((T, D), BF16), V((T, D), BF16),
-        V((D, EL), BF16), V((D, EL), BF16), V((2 * EL, D), BF16),
+        V((D, 2, EL), BF16), V((D, EL), BF16), V((D, EL), BF16), V((2 * EL, D), BF16),
         V((8, 2, 16, D), BF16), V((TB, TB), BF16),
         V((2, T + 16, EL), F32), V((2, T, EL), BF16), V((2, T, 2 * L), BF16),
-        V((2, T, EL), F32), V((2, T, EL), F32), V((2, T, EL), F32),
+        V((2, T, EL), F32), V((2, T, EL), F32),
         V((2, NC * H, L), F32), V((NC, L, L), F32), V((T, L), F32), V((2, NC, H, L), F32),
         V((2, NC, L, EL), F32), V((2, NC, L, EL), BF16),
         V((2, 16, EL), BF16), V((2, 16, EL), BF16),
@@ -502,14 +488,14 @@
         V((NB, 8, 8, TB), F32), V((T, 2 * EL), BF16), V((NB, 2, 4, TB, TB), BF16),
         V((NB, 4, XR, TB), BF16), V((NB, 4, XR, TB), BF16), V((NB, 3, XR, TB), BF16),
         V((NB, 3, 2, TB - XR, TB), BF16), V((NB, TB - XR, TB), BF16), V((NB, TB - XR, TB), BF16),
-        dma((NB,)), dma((3,)), dma, dma((7,)), dma((7,)), dma, dma, dma((2,)), dma((2,)), dma, dma, dma, dma,
+        dma((NB,)), dma((NB,)), dma, dma, dma((7,)), dma((7,)), dma, dma, dma((2,)), dma((2,)), dma, dma, dma, dma,
         dma((3,)), dma((3,)), dma, dma, dma((NB, 7)), dma((NB, 7)),
         dma((NB,)), dma((NB,)), dma((NB, 3)), dma((NB, 3)), dma((NB, 3)), dma((NB, 3)), dma((NB,)), dma((NB,)),
     ]
     return pl.pallas_call(
         kernel,
         out_shape=jax.ShapeDtypeStruct((D // 8, T), BF16),
-        in_specs=[hbm, vm, vm, hbm, hbm, hbm, vm, vm, vm, vm, hbm, sm, sm, sm],
+        in_specs=[hbm, vm, vm, hbm, hbm, vm, vm, vm, vm, hbm, sm, sm, sm],
         out_specs=vm,
         scratch_shapes=scratch,
         compiler_params=pltpu.CompilerParams(
@@ -517,8 +503,7 @@
         ),
         cost_estimate=pl.CostEstimate(flops=20_000_000_000, bytes_accessed=16_000_000, transcendentals=4_000_000),
     )(
-        hidden, ids.reshape(1, T), jnp.pad(table, ((0, 16 - table.shape[0]), (0, 0))),
-        proj_weight[:, 1, :], proj_weight[:, 0, :], bc_weight.T.reshape(2, 16, D), dt_weight.T,
+        hidden, ids.reshape(1, T), table, proj_weight, bc_weight.T.reshape(2, 16, D), dt_weight.T,
         conv_weight, conv_bias.reshape(1, EL), norm_gain.reshape(1, EL), out_weight,
         dt_bias, decay, skip,
     )

time: 107 us -> 92.9 us (0.87)
  local copies, waits for them, and re-layouts: 14.6 us -> 1.87 us
  Pallas kernels: 91.9 us -> 90.8 us
    slice x1 -> x0, local copies, waits for them, and re-layouts: 8.94 us -> none  [per_device(): proj_weight[:, 0, :]]
    squeeze x1 -> x0, local copies, waits for them, and re-layouts: 3.17 us -> none  [per_device(): proj_weight[:, 0, :]]
    pallas_call x1, Pallas kernels: 91.9 us -> 90.8 us  [per_device(): pl.pallas_call(kernel, out_shape=jax.ShapeDtypeStruct((D // 8, T), BF16),...]
where the time goes in v1:
time: 92.9 us; the launch traced here: 92.7 us
  Pallas kernels  90.8 us (98%)
  local copies, waits for them, and re-layouts  1.87 us (2%)
    pallas_call x1, Pallas kernels, per_device(): pl.pallas_call(kernel, out_shape=jax.ShapeDtypeStruct((D // 8, T), BF16),...  90.8 us
    unnamed x1, local copies, waits for them, and re-layouts  1.87 us

profile of v1, /device:TPU:0, one launch (start us, length us, event | category | flops | bytes accessed | tf_op | source)
XLA Modules:
  0.0 92.7 jit_solution(12139007323646729246)
XLA Ops:
  0.0 90.8 %shard_map.127 = bf16[256,1024]{1,0:T(8,128)(2,1)} custom-call(bf16[1024,2048]{1,0:T(8,128)(2,1)} %hid_hbm.1, s32[1,1024]{1,0:T(1,128)} %bitcast.9, bf16[5,2048]{1,0:T(8,128)(2,1)} %table_ref.1, bf16[2048,2,512]{2,1,0:T(2,128)(2,1)} %w_hbm.1, bf16[2,16,2048]{2,1,0:T(8,128)(2,1)} %bitcast.7, bf16[8,2048]{1,0:T(8,128)(2,1)} %bitcast.8, f32[4,512]{1,0:T(4,128)} %cw_ref.1, ...), custom_call_target="tpu_custom_call" | custom-call | flops 20000000000 | bytes 16000000 | tf_op jit(solution)/shard_map/pallas_call | solution.py:495
  90.8 1.9 %copy.15 = bf16[256,1024]{1,0:T(8,128)(2,1)} copy(bf16[256,1024]{1,0:T(8,128)(2,1)} %shard_map.127) | data formatting | bytes 1048576

commit v2 on v1

--- a/solution.py
+++ b/solution.py
@@ -43,10 +43,10 @@
     hid_hbm, ids_ref, table_ref, w_hbm, bcw_hbm, dtw_ref, cw_ref, cb_ref, gain_ref, wo_hbm,
     dtb_ref, decay_ref, skip_ref,
     out_ref,
-    u, ur, wraw, wx, wg, wall, bcw, flip, xin, xc, bc, gate, ybuf, dtraw, rowsbuf, cols, arow, sch, sst,
-    halo_out, halo_in, st_out, st_in, ch_out, ch_in, pl_out, pl_in, fin_out, fin_in,
+    u, ur, wraw, wx, wg, wall, bcw, flip, xin, xc, bt, ct, cm, gate, ybuf, dtraw, rowsbuf, cols, arow, sch, sst,
+    halo_out, halo_in, st_out, st_in, ch_out, ch_in, fin_out, fin_in,
     sq, nrm, part, rx, qbuf, ry, ry2, abuf, rx2,
-    hsem, wsem, wosem, bsem, bgs, bgr, bcs, bcr, hs, hr, sts, stsr, chs, chr_, pls, plr, fis, fir, sqs, sqr,
+    hsem, wsem, wosem, bsem, bgs, bgr, bcs, bcr, hs, hr, sts, stsr, chs, chr_, fis, fir, sqs, sqr,
     rxs, rxr, rys, ryr, ry2s, ry2r, rx2s, rx2r,
 ):
     T, D = u.shape
@@ -76,30 +76,33 @@
         for b in range(NB)
     ]
     woc = pltpu.make_async_copy(wo_hbm, wall.at[pl.ds(0, EL)], wosem)
-    bown = pltpu.make_async_copy(bcw_hbm.at[core], bcw.at[s, core], bsem)
+    bown = pltpu.make_async_copy(bcw_hbm.at[core], bcw.at[core * 8 + s], bsem)
+    hcopies[0].start()
     for b in range(NB):
-        hcopies[b].start()
         wcopies[b].start()
     bown.start()
+    for b in range(1, NB):
+        hcopies[b].start()
 
     mate = c + 1 - 2 * core
     other = (c + 16 + 2 * core - 1) % 16
-    xmate = c + 2 - 4 * xh
+    chip = c // 2
     barrier = pltpu.get_barrier_semaphore()
-    peers = [(mate, s), (other, s), (xmate, s)]
-    peers += [((c + 4 * k) % 16, s) for k in range(1, 4)]
+    peers = [(mate, s), (other, s)]
+    peers += [((c + 2 * k) % 16, s) for k in range(1, 8)]
     peers += [(c, (s + k) % 8) for k in range(1, 8)]
     for pc, ps in peers:
         pl.semaphore_signal(barrier, inc=1, device_id={"ctx": pc, "shard": ps}, device_id_type=MESH)
     pl.semaphore_wait(barrier, len(peers))
 
     def gather(k):
-        return remote(bcw_hbm.at[core], bcw.at[s, core], bgs.at[k - 1], bgr.at[k - 1], shard=(s + k) % 8)
+        return remote(bcw_hbm.at[core], bcw.at[core * 8 + s], bgs.at[k - 1], bgr.at[k - 1], shard=(s + k) % 8)
 
     for k in range(1, 8):
         gather(k).start()
 
     flip[...] = jnp.where(iota((TB, TB), 0) + iota((TB, TB), 1) == TB - 1, 1.0, 0.0).astype(BF16)
+    bcw[16] = jnp.concatenate([dtw_ref[...].astype(F32), jnp.zeros((16 - H, D), F32)], 0).astype(BF16)
     nd = D // TB
     for b in range(NB):
         rows = slice(b * TB, (b + 1) * TB)
@@ -111,24 +114,18 @@
             ur[rows, i * TB:(i + 1) * TB] = dot(
                 u[rows, (nd - 1 - i) * TB:(nd - i) * TB], flip[...]
             ).astype(BF16)
-        wcopies[b].wait()
-        for k in range(WR // L):
-            wr = slice(b * WR + k * L, b * WR + (k + 1) * L)
-            pair = jnp.swapaxes(wraw[wr, :, :], 0, 1)
-            wg[wr, :] = pair[0]
-            wx[wr, :] = pair[1]
-    woc.start()
-
-    PB = 512
-    for b in range(T // PB):
-        rows = slice(b * PB, (b + 1) * PB)
+        if b == 0:
+            for m in range(NB):
+                wcopies[m].wait()
+                for k in range(WR // L):
+                    wr = slice(m * WR + k * L, m * WR + (k + 1) * L)
+                    pair = jnp.swapaxes(wraw[wr, :, :], 0, 1)
+                    wg[wr, :] = pair[0]
+                    wx[wr, :] = pair[1]
         for i, v in enumerate((u, ur)):
             xv = dot(v[rows, :], wx[...]).astype(BF16)
-            xin[i, 8 + b * PB:8 + (b + 1) * PB, :] = xv.astype(F32)
-            dr = dot(dtw_ref[...], v[rows, :], NT)
-            for q in range(PB // L):
-                k = b * (PB // L) + q
-                dtraw[i, k * H:(k + 1) * H, :] = dr[:, q * L:(q + 1) * L]
+            xin[i, 8 + b * TB:8 + (b + 1) * TB, :] = xv.astype(F32)
+    woc.start()
 
     halo_out[0] = xin[0, T - 8:T + 8, :].astype(BF16)
     halo_out[1] = xin[1, 8:24, :].astype(BF16)
@@ -141,8 +138,21 @@
     bown.wait()
     for k in range(1, 8):
         gather(k).wait()
-    swap = remote(bcw.at[:, core], bcw.at[:, core], bcs, bcr, ctx=mate)
+    swap = remote(bcw.at[pl.ds(core * 8, 8)], bcw.at[pl.ds(core * 8, 8)], bcs, bcr, ctx=mate)
     swap.start()
+    swap.wait()
+
+    for b in range(NB):
+        rows = slice(b * TB, (b + 1) * TB)
+        for i, v in enumerate((u, ur)):
+            r = dot(bcw[...].reshape(17 * 16, D), v[rows, :], NT)
+            half = L // 2
+            for m in range(2):
+                bt[i, m * half:(m + 1) * half, rows] = r[m * L:m * L + half].astype(BF16)
+                ct[i, m * half:(m + 1) * half, rows] = r[m * L + half:(m + 1) * L].astype(BF16)
+            for q in range(TB // L):
+                k = b * (TB // L) + q
+                dtraw[i, k * H:(k + 1) * H, :] = r[2 * L:2 * L + H, q * L:(q + 1) * L]
 
     head = iota((NC * H, L), 0) % H
     bias = jnp.zeros((NC * H, L), F32)
@@ -185,34 +195,29 @@
     for k in range(NC):
         cols[k * L:(k + 1) * L, :] = rowsbuf[k].T
 
-    swap.wait()
-    for b in range(T // PB):
-        rows = slice(b * PB, (b + 1) * PB)
-        for i, v in enumerate((u, ur)):
-            bc[i, rows, :] = dot(v[rows, :], bcw[...].reshape(8 * 32, D), NT).astype(BF16)
-
     hcf.wait()
     hcr.wait()
     xin[0, 0:8, :] = jnp.where(c > 0, halo_in[0, 8:16, :].astype(F32), 0.0)
     xin[1, T + 8:T + 16, :] = jnp.where(c < 15, halo_in[1, 0:8, :].astype(F32), 0.0)
 
-    def chunk_state(k, _):
-        rows = rows_of(k, L)
+    half_w, half_b = 0.5 * cw_ref[...], 0.5 * cb_ref[...]
+
+    def chunk_state(k):
+        rows = slice(k * L, (k + 1) * L)
         for i in range(2):
-            window = xin[i, pl.ds(pl.multiple_of(k * L, L), L + 16), :]
-            acc = jnp.zeros((L, EL), F32) + cb_ref[...]
+            window = xin[i, k * L:(k + 1) * L + 16, :]
+            acc = jnp.zeros((L, EL), F32) + half_b
             for t in range(4):
                 at = 8 - 3 + t if i == 0 else 8 + 3 - t
-                acc = acc + cw_ref[t:t + 1, :] * window[at:at + L, :]
-            xv = silu(acc).astype(BF16)
+                acc = acc + half_w[t:t + 1, :] * window[at:at + L, :]
+            xv = (acc + acc * jnp.tanh(acc)).astype(BF16)
             xc[i, rows, :] = xv
             wexp = dot(cols[rows, :].astype(BF16), spreads[2 * i])
             scaled = (wexp * xv.astype(F32)).astype(BF16)
-            bt = bc[i, rows, 0:L].astype(F32).T.astype(BF16)
-            sch[i, k] = dot(bt, scaled)
-        return 0
-
-    lax.fori_loop(0, NC, chunk_state, 0, unroll=2)
+            sch[i, k] = dot(bt[i, :, rows], scaled)
+
+    for k in range(NC):
+        chunk_state(k)
 
     def pack_decay(d):
         hi, lo = split(d)
@@ -248,7 +253,9 @@
         for k in range(j * (TB // L), (j + 1) * (TB // L)):
             rows = slice(k * L, (k + 1) * L)
             for i in range(2):
-                cb = dot(bc[i, rows, L:2 * L], bc[i, rows, 0:L], NT)
+                cv = ct[i, :, rows].astype(F32).T.astype(BF16)
+                cm[i, rows, :] = cv
+                cb = dot(cv, bt[i, :, rows])
                 keep = iota((L, L), 0) >= lane if i == 0 else iota((L, L), 0) <= lane
                 ar = arow[i, k]
                 for q in range(H // 2):
@@ -276,49 +283,38 @@
     for i in range(2):
         ms, md = load_state(st_out.at[i, :, half])
         ts, td = load_state(st_in.at[i, :, half])
-        mine_first = core == i
-        state = jnp.where(mine_first, td * ms + ts, md * ts + ms)
+        state = jnp.where(core == i, td * ms + ts, md * ts + ms)
         ch_out[i, 0:L, :] = state.astype(BF16)
         ch_out[i, L:L + 16, :] = pack_decay(md * td)
-    cha = remote(ch_out, ch_in, chs, chr_, ctx=xmate)
-    cha.start()
+
+    def chips(k):
+        return remote(
+            ch_out.at[(chip + k) // 8], ch_in.at[chip], chs.at[k - 1], chr_.at[k - 1], ctx=(c + 2 * k) % 16
+        )
+
+    for k in range(1, 8):
+        chips(k).start()
+    ch_in[chip] = ch_out[0]
 
     late_block(0)
 
-    cha.wait()
+    late_block(1)
+
+    for k in range(1, 8):
+        chips(k).wait_send()
+        pltpu.make_async_remote_copy(
+            src_ref=ch_out.at[0], dst_ref=ch_in.at[(chip + 8 - k) % 8], send_sem=chs.at[k - 1],
+            recv_sem=chr_.at[k - 1], device_id={"ctx": (c + 2 * k) % 16, "shard": s}, device_id_type=MESH,
+        ).wait_recv()
+    entries = [jnp.zeros((L, HC), F32), jnp.zeros((L, HC), F32)]
+    for pp in range(7):
+        ps, pd = load_state(ch_in.at[pp])
+        entries[0] = jnp.where(pp < chip, pd * entries[0] + ps, entries[0])
+    for pp in range(7, 0, -1):
+        ps, pd = load_state(ch_in.at[pp])
+        entries[1] = jnp.where(pp > chip, pd * entries[1] + ps, entries[1])
     for i in range(2):
-        ms, md = load_state(ch_out.at[i])
-        ts, td = load_state(ch_in.at[i])
-        mine_first = xh == i
-        state = jnp.where(mine_first, td * ms + ts, md * ts + ms)
-        pl_out[i, 0:L, :] = state.astype(BF16)
-        pl_out[i, L:L + 16, :] = pack_decay(md * td)
-
-    def plane(k):
-        return remote(
-            pl_out.at[(z + k) // 4], pl_in.at[z], pls.at[k - 1], plr.at[k - 1], ctx=(c + 4 * k) % 16
-        )
-
-    for k in range(1, 4):
-        plane(k).start()
-    pl_in[z] = pl_out[0]
-
-    late_block(1)
-
-    for k in range(1, 4):
-        plane(k).wait_send()
-        pltpu.make_async_remote_copy(
-            src_ref=pl_out.at[0], dst_ref=pl_in.at[(z + 4 - k) % 4], send_sem=pls.at[k - 1],
-            recv_sem=plr.at[k - 1], device_id={"ctx": (c + 4 * k) % 16, "shard": s}, device_id_type=MESH,
-        ).wait_recv()
-    for i in range(2):
-        acc = jnp.zeros((L, HC), F32)
-        for zz in (range(3) if i == 0 else range(3, 0, -1)):
-            ps, pd = load_state(pl_in.at[zz])
-            acc = jnp.where((zz < z) if i == 0 else (zz > z), pd * acc + ps, acc)
-        ts, td = load_state(ch_in.at[i])
-        acc = jnp.where(xh != i, td * acc + ts, acc)
-        fin_out[i] = acc.astype(BF16)
+        fin_out[i] = entries[i].astype(BF16)
     fina = remote(fin_out, fin_in, fis, fir, ctx=mate)
     fina.start()
     fina.wait()
@@ -346,7 +342,7 @@
                 k = j * (TB // L) + q
                 rows = slice(k * L, (k + 1) * L)
                 eexp = dot(cols[rows, :].astype(BF16), spreads[2 * i + 1])
-                yv = ybuf[i, rows, :] + eexp * dot(bc[i, rows, L:2 * L], sst[i, k])
+                yv = ybuf[i, rows, :] + eexp * dot(cm[i, rows, :], sst[i, k])
                 ybuf[i, rows, :] = yv * gate[i, rows, :]
             rows = slice(j * TB, (j + 1) * TB)
             gv = ybuf[i, rows, :]
@@ -443,8 +439,8 @@
     kept = [None] * NB
     gated_block(0)
     gated_block(1)
+    late_block(2)
     product_block(0)
-    late_block(2)
     gated_block(2)
     product_block(1)
     late_block(3)
@@ -475,21 +471,20 @@
     scratch = [
         V((T, D), BF16), V((T, D), BF16),
         V((D, 2, EL), BF16), V((D, EL), BF16), V((D, EL), BF16), V((2 * EL, D), BF16),
-        V((8, 2, 16, D), BF16), V((TB, TB), BF16),
-        V((2, T + 16, EL), F32), V((2, T, EL), BF16), V((2, T, 2 * L), BF16),
+        V((17, 16, D), BF16), V((TB, TB), BF16),
+        V((2, T + 16, EL), F32), V((2, T, EL), BF16), V((2, L, T), BF16), V((2, L, T), BF16), V((2, T, L), BF16),
         V((2, T, EL), F32), V((2, T, EL), F32),
         V((2, NC * H, L), F32), V((NC, L, L), F32), V((T, L), F32), V((2, NC, H, L), F32),
         V((2, NC, L, EL), F32), V((2, NC, L, EL), BF16),
         V((2, 16, EL), BF16), V((2, 16, EL), BF16),
         V((2, L + 16, EL), BF16), V((2, L + 16, EL), BF16),
-        V((2, L + 16, EL // 2), BF16), V((2, L + 16, EL // 2), BF16),
-        V((2, L + 16, EL // 2), BF16), V((4, L + 16, EL // 2), BF16),
+        V((2, L + 16, EL // 2), BF16), V((8, L + 16, EL // 2), BF16),
         V((2, L, EL // 2), BF16), V((2, L, EL // 2), BF16),
         V((NB, 8, 8, TB), F32), V((T, 2 * EL), BF16), V((NB, 2, 4, TB, TB), BF16),
         V((NB, 4, XR, TB), BF16), V((NB, 4, XR, TB), BF16), V((NB, 3, XR, TB), BF16),
         V((NB, 3, 2, TB - XR, TB), BF16), V((NB, TB - XR, TB), BF16), V((NB, TB - XR, TB), BF16),
-        dma((NB,)), dma((NB,)), dma, dma, dma((7,)), dma((7,)), dma, dma, dma((2,)), dma((2,)), dma, dma, dma, dma,
-        dma((3,)), dma((3,)), dma, dma, dma((NB, 7)), dma((NB, 7)),
+        dma((NB,)), dma((NB,)), dma, dma, dma((7,)), dma((7,)), dma, dma, dma((2,)), dma((2,)), dma, dma, dma((7,)), dma((7,)),
+        dma, dma, dma((NB, 7)), dma((NB, 7)),
         dma((NB,)), dma((NB,)), dma((NB, 3)), dma((NB, 3)), dma((NB, 3)), dma((NB, 3)), dma((NB,)), dma((NB,)),
     ]
     return pl.pallas_call(

time: 92.9 us -> 89.1 us (0.959)
  Pallas kernels: 90.8 us -> 87 us
    pallas_call x1, Pallas kernels: 90.8 us -> 87 us  [per_device(): pl.pallas_call(kernel, out_shape=jax.ShapeDtypeStruct((D // 8, T), BF16),...]
where the time goes in v2:
time: 89.1 us; the launch traced here: 88.9 us
  Pallas kernels  87 us (98%)
  local copies, waits for them, and re-layouts  1.87 us (2%)
    pallas_call x1, Pallas kernels, per_device(): pl.pallas_call(kernel, out_shape=jax.ShapeDtypeStruct((D // 8, T), BF16),...  87 us
    unnamed x1, local copies, waits for them, and re-layouts  1.87 us

profile of v2, /device:TPU:0, one launch (start us, length us, event | category | flops | bytes accessed | tf_op | source)
XLA Modules:
  0.0 88.9 jit_solution(5254676322177818968)
XLA Ops:
  0.0 87.0 %shard_map.127 = bf16[256,1024]{1,0:T(8,128)(2,1)} custom-call(bf16[1024,2048]{1,0:T(8,128)(2,1)} %hid_hbm.1, s32[1,1024]{1,0:T(1,128)} %bitcast.9, bf16[5,2048]{1,0:T(8,128)(2,1)} %table_ref.1, bf16[2048,2,512]{2,1,0:T(2,128)(2,1)} %w_hbm.1, bf16[2,16,2048]{2,1,0:T(8,128)(2,1)} %bitcast.7, bf16[8,2048]{1,0:T(8,128)(2,1)} %bitcast.8, f32[4,512]{1,0:T(4,128)} %cw_ref.1, ...), custom_call_target="tpu_custom_call" | custom-call | flops 20000000000 | bytes 16000000 | tf_op jit(solution)/shard_map/pallas_call | solution.py:490
  87.0 1.9 %copy.15 = bf16[256,1024]{1,0:T(8,128)(2,1)} copy(bf16[256,1024]{1,0:T(8,128)(2,1)} %shard_map.127) | data formatting | bytes 1048576

commit v3 on v2

--- a/solution.py
+++ b/solution.py
@@ -8,7 +8,12 @@
 E = 4096
 L = 128
 TB = 256
-XR = 160
+BLOCKS = (
+    (0, 256, 112, 48, 80), (256, 256, 112, 48, 80), (512, 256, 112, 48, 80),
+    (768, 128, 64, 32, 32), (896, 128, 64, 32, 32),
+)
+NR = len(BLOCKS)
+XM, XH, YM, YH = 112, 64, 144, 80
 HEADDIM = 64
 MESH = pl.DeviceIdType.MESH
 F32 = jnp.float32
@@ -45,9 +50,9 @@
     out_ref,
     u, ur, wraw, wx, wg, wall, bcw, flip, xin, xc, bt, ct, cm, gate, ybuf, dtraw, rowsbuf, cols, arow, sch, sst,
     halo_out, halo_in, st_out, st_in, ch_out, ch_in, fin_out, fin_in,
-    sq, nrm, part, rx, qbuf, ry, ry2, abuf, rx2,
+    sq, nrm, part, rx, qbuf, abuf, rx2, xa, xb, xaa, xba, xprev, xnext, ya, yb, yaa, yba, yprev, ynext,
     hsem, wsem, wosem, bsem, bgs, bgr, bcs, bcr, hs, hr, sts, stsr, chs, chr_, fis, fir, sqs, sqr,
-    rxs, rxr, rys, ryr, ry2s, ry2r, rx2s, rx2r,
+    rxs, rxr, rx2s, rx2r, xss, xsr, yss, ysr,
 ):
     T, D = u.shape
     EL = xc.shape[2]
@@ -77,12 +82,11 @@
     ]
     woc = pltpu.make_async_copy(wo_hbm, wall.at[pl.ds(0, EL)], wosem)
     bown = pltpu.make_async_copy(bcw_hbm.at[core], bcw.at[core * 8 + s], bsem)
-    hcopies[0].start()
+    for b in range(NB):
+        hcopies[b].start()
     for b in range(NB):
         wcopies[b].start()
     bown.start()
-    for b in range(1, NB):
-        hcopies[b].start()
 
     mate = c + 1 - 2 * core
     other = (c + 16 + 2 * core - 1) % 16
@@ -114,17 +118,19 @@
             ur[rows, i * TB:(i + 1) * TB] = dot(
                 u[rows, (nd - 1 - i) * TB:(nd - i) * TB], flip[...]
             ).astype(BF16)
-        if b == 0:
-            for m in range(NB):
-                wcopies[m].wait()
-                for k in range(WR // L):
-                    wr = slice(m * WR + k * L, m * WR + (k + 1) * L)
-                    pair = jnp.swapaxes(wraw[wr, :, :], 0, 1)
-                    wg[wr, :] = pair[0]
-                    wx[wr, :] = pair[1]
+    for m in range(NB):
+        wcopies[m].wait()
+        for k in range(WR // L):
+            wr = slice(m * WR + k * L, m * WR + (k + 1) * L)
+            pair = jnp.swapaxes(wraw[wr, :, :], 0, 1)
+            wg[wr, :] = pair[0]
+            wx[wr, :] = pair[1]
+    PB = 512
+    for b in range(T // PB):
+        rows = slice(b * PB, (b + 1) * PB)
         for i, v in enumerate((u, ur)):
             xv = dot(v[rows, :], wx[...]).astype(BF16)
-            xin[i, 8 + b * TB:8 + (b + 1) * TB, :] = xv.astype(F32)
+            xin[i, 8 + b * PB:8 + (b + 1) * PB, :] = xv.astype(F32)
     woc.start()
 
     halo_out[0] = xin[0, T - 8:T + 8, :].astype(BF16)
@@ -140,6 +146,20 @@
         gather(k).wait()
     swap = remote(bcw.at[pl.ds(core * 8, 8)], bcw.at[pl.ds(core * 8, 8)], bcs, bcr, ctx=mate)
     swap.start()
+
+    hcf.wait()
+    hcr.wait()
+    xin[0, 0:8, :] = jnp.where(c > 0, halo_in[0, 8:16, :].astype(F32), 0.0)
+    xin[1, T + 8:T + 16, :] = jnp.where(c < 15, halo_in[1, 0:8, :].astype(F32), 0.0)
+    half_w, half_b = 0.5 * cw_ref[...], 0.5 * cb_ref[...]
+    for k in range(NC):
+        for i in range(2):
+            window = xin[i, k * L:(k + 1) * L + 16, :]
+            acc = jnp.zeros((L, EL), F32) + half_b
+            for t in range(4):
+                at = 8 - 3 + t if i == 0 else 8 + 3 - t
+                acc = acc + half_w[t:t + 1, :] * window[at:at + L, :]
+            xc[i, k * L:(k + 1) * L, :] = (acc + acc * jnp.tanh(acc)).astype(BF16)
     swap.wait()
 
     for b in range(NB):
@@ -195,29 +215,12 @@
     for k in range(NC):
         cols[k * L:(k + 1) * L, :] = rowsbuf[k].T
 
-    hcf.wait()
-    hcr.wait()
-    xin[0, 0:8, :] = jnp.where(c > 0, halo_in[0, 8:16, :].astype(F32), 0.0)
-    xin[1, T + 8:T + 16, :] = jnp.where(c < 15, halo_in[1, 0:8, :].astype(F32), 0.0)
-
-    half_w, half_b = 0.5 * cw_ref[...], 0.5 * cb_ref[...]
-
-    def chunk_state(k):
+    for k in range(NC):
         rows = slice(k * L, (k + 1) * L)
         for i in range(2):
-            window = xin[i, k * L:(k + 1) * L + 16, :]
-            acc = jnp.zeros((L, EL), F32) + half_b
-            for t in range(4):
-                at = 8 - 3 + t if i == 0 else 8 + 3 - t
-                acc = acc + half_w[t:t + 1, :] * window[at:at + L, :]
-            xv = (acc + acc * jnp.tanh(acc)).astype(BF16)
-            xc[i, rows, :] = xv
             wexp = dot(cols[rows, :].astype(BF16), spreads[2 * i])
-            scaled = (wexp * xv.astype(F32)).astype(BF16)
+            scaled = (wexp * xc[i, rows, :].astype(F32)).astype(BF16)
             sch[i, k] = dot(bt[i, :, rows], scaled)
-
-    for k in range(NC):
-        chunk_state(k)
 
     def pack_decay(d):
         hi, lo = split(d)
@@ -360,83 +363,126 @@
             ).wait_recv()
 
     xs = s + 1 - 2 * xl
+    up, down, across = (y + 1) % 4, (y + 3) % 4, (y + 2) % 4
 
     def cross(j):
+        xr = BLOCKS[j][2]
         return remote(
-            part.at[j, 1 - xl, :, pl.ds(0, XR), :], rx.at[j], rxs.at[j], rxr.at[j], shard=xs
+            part.at[j, 1 - xl, :, pl.ds(0, xr), :], rx.at[j, :, pl.ds(0, xr), :], rxs.at[j], rxr.at[j], shard=xs
         )
 
-    def along(j, k):
-        yk = (y + k) % 4
-        return remote(
-            part.at[j, :, yk, pl.ds(XR, TB - XR), :], ry2.at[j, k - 1], ry2s.at[j, k - 1], ry2r.at[j, k - 1],
-            shard=yk * 2 + xl,
-        )
-
-    def along2(j, k):
-        yk = (y + k) % 4
-        return remote(qbuf.at[j, yk], ry.at[j, k - 1], rys.at[j, k - 1], ryr.at[j, k - 1], shard=yk * 2 + xl)
-
     def cross2(j):
-        return remote(abuf.at[j], rx2.at[j], rx2s.at[j], rx2r.at[j], shard=xs)
+        n = BLOCKS[j][1] - BLOCKS[j][2]
+        return remote(abuf.at[j, pl.ds(0, n)], rx2.at[j, pl.ds(0, n)], rx2s.at[j], rx2r.at[j], shard=xs)
+
+    def ring_y(j, step):
+        n, xr, h0 = BLOCKS[j][1], BLOCKS[j][2], BLOCKS[j][4]
+        h1 = n - xr - h0
+        lo, hi = pl.ds(0, h0), pl.ds(h0, h1)
+        plo, phi = pl.ds(xr, h0), pl.ds(xr + h0, h1)
+        src, dst, to = [
+            (part.at[j, :, across, plo, :], ya.at[j, :, lo, :], up),
+            (part.at[j, :, across, phi, :], yb.at[j, :, pl.ds(0, h1), :], down),
+            (part.at[j, :, up, phi, :], yprev.at[j, :, hi, :], up),
+            (part.at[j, :, down, plo, :], ynext.at[j, :, lo, :], down),
+            (yaa.at[j, :, lo, :], yprev.at[j, :, lo, :], up),
+            (yba.at[j, :, pl.ds(0, h1), :], ynext.at[j, :, hi, :], down),
+        ][step]
+        return remote(src, dst, yss.at[j, step], ysr.at[j, step], shard=to * 2 + xl)
+
+    def ring_x(j, step):
+        xr, h0 = BLOCKS[j][2], BLOCKS[j][3]
+        h1 = xr - h0
+        lo, hi = pl.ds(0, h0), pl.ds(h0, h1)
+        src, dst, to = [
+            (qbuf.at[j, across, lo, :], xa.at[j, lo, :], up),
+            (qbuf.at[j, across, hi, :], xb.at[j, pl.ds(0, h1), :], down),
+            (qbuf.at[j, up, hi, :], xprev.at[j, hi, :], up),
+            (qbuf.at[j, down, lo, :], xnext.at[j, lo, :], down),
+            (xaa.at[j, lo, :], xprev.at[j, lo, :], up),
+            (xba.at[j, pl.ds(0, h1), :], xnext.at[j, hi, :], down),
+        ][step]
+        return remote(src, dst, xss.at[j, step], xsr.at[j, step], shard=to * 2 + xl)
 
     def product_block(j):
-        wait_sums(j)
-        total = sq[j, 0]
+        r0, n, xr = BLOCKS[j][:3]
+        tb = r0 // TB
+        if r0 % TB == 0:
+            wait_sums(tb)
+        total = sq[tb, 0]
         for k in range(1, 8):
-            total = total + sq[j, k]
+            total = total + sq[tb, k]
         scale = lax.rsqrt(total / E + 1e-05)
-        rows = slice(j * TB, (j + 1) * TB)
-        for q in range(TB // L):
-            col = jnp.concatenate([scale[:, q * L:(q + 1) * L]] * (L // 8), 0).T
-            sub = slice(j * TB + q * L, j * TB + (q + 1) * L)
+        rows = slice(r0, r0 + n)
+        for q in range(r0, r0 + n, L):
+            at = q % TB
+            col = jnp.concatenate([scale[:, at:at + L]] * (L // 8), 0).T
+            sub = slice(q, q + L)
             for i in range(2):
                 nv = ybuf[i, sub, :] * col[:, 4 * i:4 * i + 1] * gain_ref[...]
                 nrm[sub, i * EL:(i + 1) * EL] = nv.astype(BF16)
-
         for p in range(8):
             xx = lax.rem(p // 4 + 1 + xl, 2)
             yy = p % 4
-            part[j, xx, yy] = dot(nrm[rows, :], wall[:, rows_of(yy * 2 + xx, TB)]).astype(BF16)
+            part[j, xx, yy, 0:n, :] = dot(nrm[rows, :], wall[:, rows_of(yy * 2 + xx, TB)]).astype(BF16)
             if p == 3:
                 cross(j).start()
-        for k in range(1, 4):
-            along(j, k).start()
+        for step in range(4):
+            ring_y(j, step).start()
 
     def middle_block(j):
+        n, xr, h0 = BLOCKS[j][1], BLOCKS[j][2], BLOCKS[j][4]
+        h1 = n - xr - h0
         cross(j).wait()
-        for k in range(4):
-            yk = (y + k) % 4
-            both = part[j, xl, yk, 0:XR, :].astype(F32) + rx[j, yk].astype(F32)
-            qbuf[j, yk] = both.astype(BF16)
-            if k:
-                along2(j, k).start()
-        for k in range(1, 4):
-            along(j, k).wait()
+        for yk in range(4):
+            both = part[j, xl, yk, 0:xr, :].astype(F32) + rx[j, yk, 0:xr, :].astype(F32)
+            qbuf[j, yk, 0:xr, :] = both.astype(BF16)
+        for step in range(4):
+            ring_x(j, step).start()
+        for step in range(2):
+            ring_y(j, step).wait()
+        for m in range(2):
+            both = part[j, m, up, xr:xr + h0, :].astype(F32) + ya[j, m, 0:h0, :].astype(F32)
+            yaa[j, m, 0:h0, :] = both.astype(BF16)
+            both = part[j, m, down, xr + h0:n, :].astype(F32) + yb[j, m, 0:h1, :].astype(F32)
+            yba[j, m, 0:h1, :] = both.astype(BF16)
+        for step in range(4, 6):
+            ring_y(j, step).start()
+
+    def third_block(j):
+        n, xr, h0 = BLOCKS[j][1:4]
+        h1 = xr - h0
+        for step in range(2):
+            ring_x(j, step).wait()
+        both = qbuf[j, up, 0:h0, :].astype(F32) + xa[j, 0:h0, :].astype(F32)
+        xaa[j, 0:h0, :] = both.astype(BF16)
+        both = qbuf[j, down, h0:xr, :].astype(F32) + xb[j, 0:h1, :].astype(F32)
+        xba[j, 0:h1, :] = both.astype(BF16)
+        for step in range(4, 6):
+            ring_x(j, step).start()
+        for step in range(2, 6):
+            ring_y(j, step).wait()
+        sums_ = []
         for m in range(2):
             xx = (xl + 1 + m) % 2
-            acc = part[j, xx, y, XR:TB, :].astype(F32)
-            for k in range(1, 4):
-                acc = acc + ry2[j, k - 1, xx].astype(F32)
-            if m == 0:
-                abuf[j] = acc.astype(BF16)
-                cross2(j).start()
-            else:
-                keepbuf = acc
-        return keepbuf
+            acc = part[j, xx, y, xr:n, :].astype(F32)
+            acc = acc + yprev[j, xx, 0:n - xr, :].astype(F32) + ynext[j, xx, 0:n - xr, :].astype(F32)
+            sums_.append(acc)
+        abuf[j, 0:n - xr, :] = sums_[0].astype(BF16)
+        cross2(j).start()
+        return sums_[1]
 
     def last_block(j, own):
-        for k in range(1, 4):
-            along2(j, k).wait()
-        acc = qbuf[j, y].astype(F32)
-        for k in range(1, 4):
-            acc = acc + ry[j, k - 1].astype(F32)
+        r0, n, xr = BLOCKS[j][:3]
+        for step in range(2, 6):
+            ring_x(j, step).wait()
+        acc = qbuf[j, y, 0:xr, :].astype(F32)
+        acc = acc + xprev[j, 0:xr, :].astype(F32) + xnext[j, 0:xr, :].astype(F32)
         cross2(j).wait()
-        low = own + rx2[j].astype(F32)
-        whole = jnp.concatenate([acc, low], 0)
-        out_ref[:, j * TB:(j + 1) * TB] = whole.T.astype(BF16)
-
-    kept = [None] * NB
+        low = own + rx2[j, 0:n - xr, :].astype(F32)
+        out_ref[:, r0:r0 + n] = jnp.concatenate([acc, low], 0).T.astype(BF16)
+
+    kept = [None] * len(BLOCKS)
     gated_block(0)
     gated_block(1)
     late_block(2)
@@ -445,14 +491,24 @@
     product_block(1)
     late_block(3)
     gated_block(3)
-    kept[0] = middle_block(0)
+    middle_block(0)
     product_block(2)
-    kept[1] = middle_block(1)
+    middle_block(1)
+    kept[0] = third_block(0)
     product_block(3)
-    kept[2] = middle_block(2)
-    kept[3] = middle_block(3)
-    for j in range(NB):
-        last_block(j, kept[j])
+    middle_block(2)
+    kept[1] = third_block(1)
+    product_block(4)
+    last_block(0, kept[0])
+    middle_block(3)
+    kept[2] = third_block(2)
+    middle_block(4)
+    last_block(1, kept[1])
+    kept[3] = third_block(3)
+    kept[4] = third_block(4)
+    last_block(2, kept[2])
+    last_block(3, kept[3])
+    last_block(4, kept[4])
 
 
 def per_device(
@@ -480,12 +536,15 @@
         V((2, L + 16, EL), BF16), V((2, L + 16, EL), BF16),
         V((2, L + 16, EL // 2), BF16), V((8, L + 16, EL // 2), BF16),
         V((2, L, EL // 2), BF16), V((2, L, EL // 2), BF16),
-        V((NB, 8, 8, TB), F32), V((T, 2 * EL), BF16), V((NB, 2, 4, TB, TB), BF16),
-        V((NB, 4, XR, TB), BF16), V((NB, 4, XR, TB), BF16), V((NB, 3, XR, TB), BF16),
-        V((NB, 3, 2, TB - XR, TB), BF16), V((NB, TB - XR, TB), BF16), V((NB, TB - XR, TB), BF16),
+        V((NB, 8, 8, TB), F32), V((T, 2 * EL), BF16), V((NR, 2, 4, TB, TB), BF16),
+        V((NR, 4, XM, TB), BF16), V((NR, 4, XM, TB), BF16), V((NR, YM, TB), BF16), V((NR, YM, TB), BF16),
+        V((NR, XH, TB), BF16), V((NR, XH, TB), BF16), V((NR, XH, TB), BF16), V((NR, XH, TB), BF16),
+        V((NR, XM, TB), BF16), V((NR, XM, TB), BF16),
+        V((NR, 2, YH, TB), BF16), V((NR, 2, YH, TB), BF16), V((NR, 2, YH, TB), BF16), V((NR, 2, YH, TB), BF16),
+        V((NR, 2, YM, TB), BF16), V((NR, 2, YM, TB), BF16),
         dma((NB,)), dma((NB,)), dma, dma, dma((7,)), dma((7,)), dma, dma, dma((2,)), dma((2,)), dma, dma, dma((7,)), dma((7,)),
         dma, dma, dma((NB, 7)), dma((NB, 7)),
-        dma((NB,)), dma((NB,)), dma((NB, 3)), dma((NB, 3)), dma((NB, 3)), dma((NB, 3)), dma((NB,)), dma((NB,)),
+        dma((NR,)), dma((NR,)), dma((NR,)), dma((NR,)), dma((NR, 6)), dma((NR, 6)), dma((NR, 6)), dma((NR, 6)),
     ]
     return pl.pallas_call(
         kernel,

time: 89.1 us -> 88.2 us (0.990)
  Pallas kernels: 87 us -> 86.1 us
    pallas_call x1, Pallas kernels: 87 us -> 86.1 us  [per_device(): pl.pallas_call(kernel, out_shape=jax.ShapeDtypeStruct((D // 8, T), BF16),...]
where the time goes in v3:
time: 88.2 us; the launch traced here: 88 us
  Pallas kernels  86.1 us (98%)
  local copies, waits for them, and re-layouts  1.87 us (2%)
    pallas_call x1, Pallas kernels, per_device(): pl.pallas_call(kernel, out_shape=jax.ShapeDtypeStruct((D // 8, T), BF16),...  86.1 us
    unnamed x1, local copies, waits for them, and re-layouts  1.87 us

profile of v3, /device:TPU:0, one launch (start us, length us, event | category | flops | bytes accessed | tf_op | source)
XLA Modules:
  0.0 88.0 jit_solution(15161378057898894286)
XLA Ops:
  0.0 86.1 %shard_map.127 = bf16[256,1024]{1,0:T(8,128)(2,1)} custom-call(bf16[1024,2048]{1,0:T(8,128)(2,1)} %hid_hbm.1, s32[1,1024]{1,0:T(1,128)} %bitcast.9, bf16[5,2048]{1,0:T(8,128)(2,1)} %table_ref.1, bf16[2048,2,512]{2,1,0:T(2,128)(2,1)} %w_hbm.1, bf16[2,16,2048]{2,1,0:T(8,128)(2,1)} %bitcast.7, bf16[8,2048]{1,0:T(8,128)(2,1)} %bitcast.8, f32[4,512]{1,0:T(4,128)} %cw_ref.1, ...), custom_call_target="tpu_custom_call" | custom-call | flops 20000000000 | bytes 16000000 | tf_op jit(solution)/shard_map/pallas_call | solution.py:549
  86.1 1.9 %copy.15 = bf16[256,1024]{1,0:T(8,128)(2,1)} copy(bf16[256,1024]{1,0:T(8,128)(2,1)} %shard_map.127) | data formatting | bytes 1048576

commit v4 on v3

--- a/solution.py
+++ b/solution.py
@@ -48,7 +48,7 @@
     hid_hbm, ids_ref, table_ref, w_hbm, bcw_hbm, dtw_ref, cw_ref, cb_ref, gain_ref, wo_hbm,
     dtb_ref, decay_ref, skip_ref,
     out_ref,
-    u, ur, wraw, wx, wg, wall, bcw, flip, xin, xc, bt, ct, cm, gate, ybuf, dtraw, rowsbuf, cols, arow, sch, sst,
+    u, ur, wraw, wx, wg, wall, bcw, flip, xin, xc, bt, ct, cm, gate, ybuf, dtraw, rowsbuf, cols, arow, sch, enter,
     halo_out, halo_in, st_out, st_in, ch_out, ch_in, fin_out, fin_in,
     sq, nrm, part, rx, qbuf, abuf, rx2, xa, xb, xaa, xba, xprev, xnext, ya, yb, yaa, yba, yprev, ynext,
     hsem, wsem, wosem, bsem, bgs, bgr, bcs, bcr, hs, hr, sts, stsr, chs, chr_, fis, fir, sqs, sqr,
@@ -100,7 +100,7 @@
     pl.semaphore_wait(barrier, len(peers))
 
     def gather(k):
-        return remote(bcw_hbm.at[core], bcw.at[core * 8 + s], bgs.at[k - 1], bgr.at[k - 1], shard=(s + k) % 8)
+        return remote(bcw_hbm.at[core], bcw.at[core * 8 + s], bgs.at[k - 1], bgr.at[s], shard=(s + k) % 8)
 
     for k in range(1, 8):
         gather(k).start()
@@ -141,38 +141,55 @@
     hcf.start()
     hcr.start()
 
+    def swap(m):
+        at = pl.ds(core * 8 + 4 * m, 4)
+        return remote(bcw.at[at], bcw.at[at], bcs.at[m], bcr.at[m], ctx=mate)
+
     bown.wait()
+    for m in range(2):
+        for src in range(4 * m, 4 * m + 4):
+            @pl.when(s != src)
+            def _():
+                remote(
+                    bcw_hbm.at[core], bcw.at[core * 8 + src], bgs.at[0], bgr.at[src], shard=(s + 1) % 8
+                ).wait_recv()
+        swap(m).start()
     for k in range(1, 8):
-        gather(k).wait()
-    swap = remote(bcw.at[pl.ds(core * 8, 8)], bcw.at[pl.ds(core * 8, 8)], bcs, bcr, ctx=mate)
-    swap.start()
-
-    hcf.wait()
-    hcr.wait()
-    xin[0, 0:8, :] = jnp.where(c > 0, halo_in[0, 8:16, :].astype(F32), 0.0)
-    xin[1, T + 8:T + 16, :] = jnp.where(c < 15, halo_in[1, 0:8, :].astype(F32), 0.0)
+        gather(k).wait_send()
+
     half_w, half_b = 0.5 * cw_ref[...], 0.5 * cb_ref[...]
+
+    def convolve(i, k):
+        window = xin[i, k * L:(k + 1) * L + 16, :]
+        acc = jnp.zeros((L, EL), F32) + half_b
+        for t in range(4):
+            at = 8 - 3 + t if i == 0 else 8 + 3 - t
+            acc = acc + half_w[t:t + 1, :] * window[at:at + L, :]
+        xc[i, k * L:(k + 1) * L, :] = (acc + acc * jnp.tanh(acc)).astype(BF16)
+
     for k in range(NC):
-        for i in range(2):
-            window = xin[i, k * L:(k + 1) * L + 16, :]
-            acc = jnp.zeros((L, EL), F32) + half_b
-            for t in range(4):
-                at = 8 - 3 + t if i == 0 else 8 + 3 - t
-                acc = acc + half_w[t:t + 1, :] * window[at:at + L, :]
-            xc[i, k * L:(k + 1) * L, :] = (acc + acc * jnp.tanh(acc)).astype(BF16)
-    swap.wait()
-
+        if k > 0:
+            convolve(0, k)
+        if k < NC - 1:
+            convolve(1, k)
+
+    def gate_block(j):
+        rows = slice(j * TB, (j + 1) * TB)
+        for i, v in enumerate((u, ur)):
+            gate[i, rows, :] = silu(dot(v[rows, :], wg[...]))
+
+    gate_block(0)
+    swap(0).wait()
+
+    wb = jnp.concatenate([bcw[0:4], bcw[8:12], bcw[16:17]], 0).reshape(L + 16, D)
     for b in range(NB):
         rows = slice(b * TB, (b + 1) * TB)
         for i, v in enumerate((u, ur)):
-            r = dot(bcw[...].reshape(17 * 16, D), v[rows, :], NT)
-            half = L // 2
-            for m in range(2):
-                bt[i, m * half:(m + 1) * half, rows] = r[m * L:m * L + half].astype(BF16)
-                ct[i, m * half:(m + 1) * half, rows] = r[m * L + half:(m + 1) * L].astype(BF16)
+            r = dot(wb, v[rows, :], NT)
+            bt[i, :, rows] = r[0:L].astype(BF16)
             for q in range(TB // L):
                 k = b * (TB // L) + q
-                dtraw[i, k * H:(k + 1) * H, :] = r[2 * L:2 * L + H, q * L:(q + 1) * L]
+                dtraw[i, k * H:(k + 1) * H, :] = r[L:L + H, q * L:(q + 1) * L]
 
     head = iota((NC * H, L), 0) % H
     bias = jnp.zeros((NC * H, L), F32)
@@ -215,6 +232,12 @@
     for k in range(NC):
         cols[k * L:(k + 1) * L, :] = rowsbuf[k].T
 
+    hcf.wait()
+    hcr.wait()
+    xin[0, 0:8, :] = jnp.where(c > 0, halo_in[0, 8:16, :].astype(F32), 0.0)
+    xin[1, T + 8:T + 16, :] = jnp.where(c < 15, halo_in[1, 0:8, :].astype(F32), 0.0)
+    convolve(0, 0)
+    convolve(1, NC - 1)
     for k in range(NC):
         rows = slice(k * L, (k + 1) * L)
         for i in range(2):
@@ -232,12 +255,15 @@
         tail = whole[L:L + 16].astype(F32)
         return whole[:L].astype(F32), tail[0:1] + tail[8:9]
 
+    reach = [[None] * NC, [None] * NC]
     for i in range(2):
-        state, dec = None, None
+        state, dec = jnp.zeros((L, EL), F32), jnp.ones((1, EL), F32)
         for k in (range(NC) if i == 0 else range(NC - 1, -1, -1)):
-            d = decs[i][k]
-            state = sch[i, k] if state is None else d * state + sch[i, k]
-            dec = d if dec is None else dec * d
+            reach[i][k] = dec
+            own = sch[i, k]
+            sch[i, k] = state
+            state = decs[i][k] * state + own
+            dec = dec * decs[i][k]
         st_out[i, 0:L, :] = state.astype(BF16)
         st_out[i, L:L + 16, :] = pack_decay(dec)
 
@@ -250,9 +276,8 @@
         sk = jnp.where(iota((1, EL), 1) // HEADDIM == h, skip_ref[h], sk)
 
     def late_block(j):
-        rows = slice(j * TB, (j + 1) * TB)
-        for i, v in enumerate((u, ur)):
-            gate[i, rows, :] = silu(dot(v[rows, :], wg[...]))
+        if j > 0:
+            gate_block(j)
         for k in range(j * (TB // L), (j + 1) * (TB // L)):
             rows = slice(k * L, (k + 1) * L)
             for i in range(2):
@@ -274,6 +299,13 @@
                     yq = dot(jnp.concatenate(ms, 1), jnp.concatenate([left, right], 0))
                     ybuf[i, rows, q * L:(q + 1) * L] = yq + sk[:, q * L:(q + 1) * L] * xp.astype(F32)
 
+    swap(1).wait()
+    wc = jnp.concatenate([bcw[4:8], bcw[12:16]], 0).reshape(L, D)
+    for b in range(NB):
+        rows = slice(b * TB, (b + 1) * TB)
+        for i, v in enumerate((u, ur)):
+            ct[i, :, rows] = dot(wc, v[rows, :], NT).astype(BF16)
+
     woc.wait()
     for i in range(nd):
         wall[EL:2 * EL, i * TB:(i + 1) * TB] = dot(
@@ -302,6 +334,7 @@
     late_block(0)
 
     late_block(1)
+    late_block(2)
 
     for k in range(1, 8):
         chips(k).wait_send()
@@ -328,11 +361,7 @@
             core == 0, jnp.concatenate([mine, theirs], 1), jnp.concatenate([theirs, mine], 1)
         )
         ts, td = load_state(st_in.at[i])
-        state = jnp.where(core != i, td * entering + ts, entering)
-        order = range(NC) if i == 0 else range(NC - 1, -1, -1)
-        for k in order:
-            sst[i, k] = state.astype(BF16)
-            state = decs[i][k] * state + sch[i, k]
+        enter[i] = jnp.where(core != i, td * entering + ts, entering)
 
     def sums(j, k):
         return remote(sq.at[j, s], sq.at[j, s], sqs.at[j, k - 1], sqr.at[j, k - 1], shard=(s + k) % 8)
@@ -345,7 +374,7 @@
                 k = j * (TB // L) + q
                 rows = slice(k * L, (k + 1) * L)
                 eexp = dot(cols[rows, :].astype(BF16), spreads[2 * i + 1])
-                yv = ybuf[i, rows, :] + eexp * dot(cm[i, rows, :], sst[i, k])
+                yv = ybuf[i, rows, :] + eexp * dot(cm[i, rows, :], (sch[i, k] + reach[i][k] * enter[i]).astype(BF16))
                 ybuf[i, rows, :] = yv * gate[i, rows, :]
             rows = slice(j * TB, (j + 1) * TB)
             gv = ybuf[i, rows, :]
@@ -480,16 +509,15 @@
         acc = acc + xprev[j, 0:xr, :].astype(F32) + xnext[j, 0:xr, :].astype(F32)
         cross2(j).wait()
         low = own + rx2[j, 0:n - xr, :].astype(F32)
-        out_ref[:, r0:r0 + n] = jnp.concatenate([acc, low], 0).T.astype(BF16)
+        out_ref[:, r0:r0 + n] = jnp.concatenate([acc, low], 0).T
 
     kept = [None] * len(BLOCKS)
     gated_block(0)
     gated_block(1)
-    late_block(2)
+    late_block(3)
     product_block(0)
     gated_block(2)
     product_block(1)
-    late_block(3)
     gated_block(3)
     middle_block(0)
     product_block(2)
@@ -531,7 +559,7 @@
         V((2, T + 16, EL), F32), V((2, T, EL), BF16), V((2, L, T), BF16), V((2, L, T), BF16), V((2, T, L), BF16),
         V((2, T, EL), F32), V((2, T, EL), F32),
         V((2, NC * H, L), F32), V((NC, L, L), F32), V((T, L), F32), V((2, NC, H, L), F32),
-        V((2, NC, L, EL), F32), V((2, NC, L, EL), BF16),
+        V((2, NC, L, EL), F32), V((2, L, EL), F32),
         V((2, 16, EL), BF16), V((2, 16, EL), BF16),
         V((2, L + 16, EL), BF16), V((2, L + 16, EL), BF16),
         V((2, L + 16, EL // 2), BF16), V((8, L + 16, EL // 2), BF16),
@@ -542,13 +570,13 @@
         V((NR, XM, TB), BF16), V((NR, XM, TB), BF16),
         V((NR, 2, YH, TB), BF16), V((NR, 2, YH, TB), BF16), V((NR, 2, YH, TB), BF16), V((NR, 2, YH, TB), BF16),
         V((NR, 2, YM, TB), BF16), V((NR, 2, YM, TB), BF16),
-        dma((NB,)), dma((NB,)), dma, dma, dma((7,)), dma((7,)), dma, dma, dma((2,)), dma((2,)), dma, dma, dma((7,)), dma((7,)),
+        dma((NB,)), dma((NB,)), dma, dma, dma((7,)), dma((8,)), dma((2,)), dma((2,)), dma((2,)), dma((2,)), dma, dma, dma((7,)), dma((7,)),
         dma, dma, dma((NB, 7)), dma((NB, 7)),
         dma((NR,)), dma((NR,)), dma((NR,)), dma((NR,)), dma((NR, 6)), dma((NR, 6)), dma((NR, 6)), dma((NR, 6)),
     ]
     return pl.pallas_call(
         kernel,
-        out_shape=jax.ShapeDtypeStruct((D // 8, T), BF16),
+        out_shape=jax.ShapeDtypeStruct((D // 8, T), F32),
         in_specs=[hbm, vm, vm, hbm, hbm, vm, vm, vm, vm, hbm, sm, sm, sm],
         out_specs=vm,
         scratch_shapes=scratch,
@@ -560,7 +588,7 @@
         hidden, ids.reshape(1, T), table, proj_weight, bc_weight.T.reshape(2, 16, D), dt_weight.T,
         conv_weight, conv_bias.reshape(1, EL), norm_gain.reshape(1, EL), out_weight,
         dt_bias, decay, skip,
-    )
+    ).astype(BF16)
 
 
 def solution(mesh):

time: 88.2 us -> 88.1 us (level)
  other arithmetic: 0 us -> 2.1 us
  local copies, waits for them, and re-layouts: 1.87 us -> 0 us
    convert_element_type x0 -> x1, other arithmetic: none -> 2.1 us  [per_device(): return pl.pallas_call(kernel, out_shape=jax.ShapeDtypeStruct((D // 8, T),...]
    unnamed x1 -> x0, local copies, waits for them, and re-layouts: 1.87 us -> none
where the time goes in v4:
time: 88.1 us; the launch traced here: 87.9 us
  Pallas kernels  85.8 us (97%)
  other arithmetic  2.1 us (2%)
    pallas_call x1, Pallas kernels, per_device(): pl.pallas_call(kernel, out_shape=jax.ShapeDtypeStruct((D // 8, T), F32),...  85.8 us
    convert_element_type x1, other arithmetic, per_device(): return pl.pallas_call(kernel, out_shape=jax.ShapeDtypeStruct((D // 8, T),...  2.1 us

profile of v4, /device:TPU:0, one launch (start us, length us, event | category | flops | bytes accessed | tf_op | source)
XLA Modules:
  0.0 87.9 jit_solution(16861621403295388227)
XLA Ops:
  0.0 85.8 %shard_map.127 = f32[256,1024]{1,0:T(8,128)} custom-call(bf16[1024,2048]{1,0:T(8,128)(2,1)} %hid_hbm.1, s32[1,1024]{1,0:T(1,128)} %bitcast.9, bf16[5,2048]{1,0:T(8,128)(2,1)} %table_ref.1, bf16[2048,2,512]{2,1,0:T(2,128)(2,1)} %w_hbm.1, bf16[2,16,2048]{2,1,0:T(8,128)(2,1)} %bitcast.7, bf16[8,2048]{1,0:T(8,128)(2,1)} %bitcast.8, f32[4,512]{1,0:T(4,128)} %cw_ref.1, ...), custom_call_target="tpu_custom_call" | custom-call | flops 20000000000 | bytes 16000000 | tf_op jit(solution)/shard_map/pallas_call | solution.py:577
  85.8 2.1 %convert_element_type.3 = bf16[256,1024]{1,0:T(8,128)(2,1)} convert(f32[256,1024]{1,0:T(8,128)} %shard_map.127) | non-fusion elementwise | flops 262144 | bytes 1572864 | tf_op jit(solution)/shard_map/convert_element_type | solution.py:591

commit v5 on v4

--- a/solution.py
+++ b/solution.py
@@ -48,11 +48,11 @@
     hid_hbm, ids_ref, table_ref, w_hbm, bcw_hbm, dtw_ref, cw_ref, cb_ref, gain_ref, wo_hbm,
     dtb_ref, decay_ref, skip_ref,
     out_ref,
-    u, ur, wraw, wx, wg, wall, bcw, flip, xin, xc, bt, ct, cm, gate, ybuf, dtraw, rowsbuf, cols, arow, sch, enter,
+    u, wraw, wx, wg, wall, bcw, lhs, ob, flip, xin, xc, bt, ct, cm, gate, ybuf, dtraw, rowsbuf, cols, arow, sch, enter,
     halo_out, halo_in, st_out, st_in, ch_out, ch_in, fin_out, fin_in,
     sq, nrm, part, rx, qbuf, abuf, rx2, xa, xb, xaa, xba, xprev, xnext, ya, yb, yaa, yba, yprev, ynext,
     hsem, wsem, wosem, bsem, bgs, bgr, bcs, bcr, hs, hr, sts, stsr, chs, chr_, fis, fir, sqs, sqr,
-    rxs, rxr, rx2s, rx2r, xss, xsr, yss, ysr,
+    rxs, rxr, rx2s, rx2r, osem, xss, xsr, yss, ysr,
 ):
     T, D = u.shape
     EL = xc.shape[2]
@@ -108,28 +108,34 @@
     flip[...] = jnp.where(iota((TB, TB), 0) + iota((TB, TB), 1) == TB - 1, 1.0, 0.0).astype(BF16)
     bcw[16] = jnp.concatenate([dtw_ref[...].astype(F32), jnp.zeros((16 - H, D), F32)], 0).astype(BF16)
     nd = D // TB
+
+    def mirror_rows(w, i):
+        w[1, (nd - 1 - i) * TB:(nd - i) * TB, :] = dot(flip[...], w[0, i * TB:(i + 1) * TB, :]).astype(BF16)
+
+    def mirror_columns(v):
+        parts = [dot(v[:, (nd - 1 - i) * TB:(nd - i) * TB], flip[...]).astype(BF16) for i in range(nd)]
+        return jnp.concatenate(parts, 1)
+
     for b in range(NB):
         rows = slice(b * TB, (b + 1) * TB)
         hcopies[b].wait()
         hot = jnp.where(iota((table_ref.shape[0], TB), 0) == ids_ref[:, rows], 1.0, 0.0).astype(BF16)
         added = dot(hot, table_ref[...], TN)
         u[rows, :] = (u[rows, :].astype(F32) + added).astype(BF16)
-        for i in range(nd):
-            ur[rows, i * TB:(i + 1) * TB] = dot(
-                u[rows, (nd - 1 - i) * TB:(nd - i) * TB], flip[...]
-            ).astype(BF16)
     for m in range(NB):
         wcopies[m].wait()
         for k in range(WR // L):
             wr = slice(m * WR + k * L, m * WR + (k + 1) * L)
             pair = jnp.swapaxes(wraw[wr, :, :], 0, 1)
-            wg[wr, :] = pair[0]
-            wx[wr, :] = pair[1]
+            wg[0, wr, :] = pair[0]
+            wx[0, wr, :] = pair[1]
+        for i in range(m * WR // TB, (m + 1) * WR // TB):
+            mirror_rows(wx, i)
     PB = 512
     for b in range(T // PB):
         rows = slice(b * PB, (b + 1) * PB)
-        for i, v in enumerate((u, ur)):
-            xv = dot(v[rows, :], wx[...]).astype(BF16)
+        for i in range(2):
+            xv = dot(u[rows, :], wx[i]).astype(BF16)
             xin[i, 8 + b * PB:8 + (b + 1) * PB, :] = xv.astype(F32)
     woc.start()
 
@@ -175,17 +181,19 @@
 
     def gate_block(j):
         rows = slice(j * TB, (j + 1) * TB)
-        for i, v in enumerate((u, ur)):
-            gate[i, rows, :] = silu(dot(v[rows, :], wg[...]))
-
-    gate_block(0)
+        for i in range(2):
+            gate[i, rows, :] = silu(dot(u[rows, :], wg[i]))
+
     swap(0).wait()
 
     wb = jnp.concatenate([bcw[0:4], bcw[8:12], bcw[16:17]], 0).reshape(L + 16, D)
+    lhs[0:L + 16, :] = wb
+    lhs[L + 16:2 * (L + 16), :] = mirror_columns(wb)
     for b in range(NB):
         rows = slice(b * TB, (b + 1) * TB)
-        for i, v in enumerate((u, ur)):
-            r = dot(wb, v[rows, :], NT)
+        both = dot(lhs[...], u[rows, :], NT)
+        for i in range(2):
+            r = both[i * (L + 16):(i + 1) * (L + 16)]
             bt[i, :, rows] = r[0:L].astype(BF16)
             for q in range(TB // L):
                 k = b * (TB // L) + q
@@ -236,11 +244,11 @@
     hcr.wait()
     xin[0, 0:8, :] = jnp.where(c > 0, halo_in[0, 8:16, :].astype(F32), 0.0)
     xin[1, T + 8:T + 16, :] = jnp.where(c < 15, halo_in[1, 0:8, :].astype(F32), 0.0)
-    convolve(0, 0)
-    convolve(1, NC - 1)
-    for k in range(NC):
-        rows = slice(k * L, (k + 1) * L)
-        for i in range(2):
+
+    def chunk_states(i):
+        convolve(i, 0 if i == 0 else NC - 1)
+        for k in range(NC):
+            rows = slice(k * L, (k + 1) * L)
             wexp = dot(cols[rows, :].astype(BF16), spreads[2 * i])
             scaled = (wexp * xc[i, rows, :].astype(F32)).astype(BF16)
             sch[i, k] = dot(bt[i, :, rows], scaled)
@@ -256,7 +264,8 @@
         return whole[:L].astype(F32), tail[0:1] + tail[8:9]
 
     reach = [[None] * NC, [None] * NC]
-    for i in range(2):
+
+    def device_state(i):
         state, dec = jnp.zeros((L, EL), F32), jnp.ones((1, EL), F32)
         for k in (range(NC) if i == 0 else range(NC - 1, -1, -1)):
             reach[i][k] = dec
@@ -267,8 +276,34 @@
         st_out[i, 0:L, :] = state.astype(BF16)
         st_out[i, L:L + 16, :] = pack_decay(dec)
 
-    sta = remote(st_out, st_in, sts, stsr, ctx=mate)
-    sta.start()
+    def mates(i):
+        return remote(st_out.at[i], st_in.at[i], sts.at[i], stsr.at[i], ctx=mate)
+
+    HC = EL // 2
+    half = pl.ds(pl.multiple_of(core * HC, HC), HC)
+
+    def chips(k, i):
+        return remote(ch_out.at[i], ch_in.at[chip], chs.at[k - 1], chr_.at[k - 1], ctx=(c + 2 * k) % 16)
+
+    def chip_state(i):
+        mates(i).wait()
+        ms, md = load_state(st_out.at[i, :, half])
+        ts, td = load_state(st_in.at[i, :, half])
+        state = jnp.where(core == i, td * ms + ts, md * ts + ms)
+        ch_out[i, 0:L, :] = state.astype(BF16)
+        ch_out[i, L:L + 16, :] = pack_decay(md * td)
+        for k in range(1, 8):
+            @pl.when((chip + k) // 8 == i)
+            def _():
+                chips(k, i).start()
+
+    chunk_states(0)
+    device_state(0)
+    mates(0).start()
+    chunk_states(1)
+    chip_state(0)
+    device_state(1)
+    mates(1).start()
 
     lane = iota((L, L), 1)
     sk = jnp.zeros((1, EL), F32)
@@ -276,8 +311,7 @@
         sk = jnp.where(iota((1, EL), 1) // HEADDIM == h, skip_ref[h], sk)
 
     def late_block(j):
-        if j > 0:
-            gate_block(j)
+        gate_block(j)
         for k in range(j * (TB // L), (j + 1) * (TB // L)):
             rows = slice(k * L, (k + 1) * L)
             for i in range(2):
@@ -301,10 +335,17 @@
 
     swap(1).wait()
     wc = jnp.concatenate([bcw[4:8], bcw[12:16]], 0).reshape(L, D)
+    lhs[0:L, :] = wc
+    lhs[L:2 * L, :] = mirror_columns(wc)
+    for i in range(nd):
+        mirror_rows(wg, i)
+    chip_state(1)
+    ch_in[chip] = ch_out[0]
     for b in range(NB):
         rows = slice(b * TB, (b + 1) * TB)
-        for i, v in enumerate((u, ur)):
-            ct[i, :, rows] = dot(wc, v[rows, :], NT).astype(BF16)
+        both = dot(lhs[0:2 * L, :], u[rows, :], NT)
+        for i in range(2):
+            ct[i, :, rows] = both[i * L:(i + 1) * L].astype(BF16)
 
     woc.wait()
     for i in range(nd):
@@ -312,32 +353,13 @@
             wall[0:EL, (nd - 1 - i) * TB:(nd - i) * TB], flip[...]
         ).astype(BF16)
 
-    sta.wait()
-    HC = EL // 2
-    half = pl.ds(pl.multiple_of(core * HC, HC), HC)
-    for i in range(2):
-        ms, md = load_state(st_out.at[i, :, half])
-        ts, td = load_state(st_in.at[i, :, half])
-        state = jnp.where(core == i, td * ms + ts, md * ts + ms)
-        ch_out[i, 0:L, :] = state.astype(BF16)
-        ch_out[i, L:L + 16, :] = pack_decay(md * td)
-
-    def chips(k):
-        return remote(
-            ch_out.at[(chip + k) // 8], ch_in.at[chip], chs.at[k - 1], chr_.at[k - 1], ctx=(c + 2 * k) % 16
-        )
-
-    for k in range(1, 8):
-        chips(k).start()
-    ch_in[chip] = ch_out[0]
-
     late_block(0)
 
     late_block(1)
     late_block(2)
 
     for k in range(1, 8):
-        chips(k).wait_send()
+        chips(k, 0).wait_send()
         pltpu.make_async_remote_copy(
             src_ref=ch_out.at[0], dst_ref=ch_in.at[(chip + 8 - k) % 8], send_sem=chs.at[k - 1],
             recv_sem=chr_.at[k - 1], device_id={"ctx": (c + 2 * k) % 16, "shard": s}, device_id_type=MESH,
@@ -509,7 +531,12 @@
         acc = acc + xprev[j, 0:xr, :].astype(F32) + xnext[j, 0:xr, :].astype(F32)
         cross2(j).wait()
         low = own + rx2[j, 0:n - xr, :].astype(F32)
-        out_ref[:, r0:r0 + n] = jnp.concatenate([acc, low], 0).T
+        ob[:, r0:r0 + n] = jnp.concatenate([acc, low], 0).T.astype(BF16)
+        leave(j).start()
+
+    def leave(j):
+        at = pl.ds(BLOCKS[j][0], BLOCKS[j][1])
+        return pltpu.make_async_copy(ob.at[:, at], out_ref.at[:, at], osem.at[j])
 
     kept = [None] * len(BLOCKS)
     gated_block(0)
@@ -537,6 +564,8 @@
     last_block(2, kept[2])
     last_block(3, kept[3])
     last_block(4, kept[4])
+    for j in range(NR):
+        leave(j).wait()
 
 
 def per_device(
@@ -553,9 +582,9 @@
     V = pltpu.VMEM
     dma = pltpu.SemaphoreType.DMA
     scratch = [
-        V((T, D), BF16), V((T, D), BF16),
-        V((D, 2, EL), BF16), V((D, EL), BF16), V((D, EL), BF16), V((2 * EL, D), BF16),
-        V((17, 16, D), BF16), V((TB, TB), BF16),
+        V((T, D), BF16),
+        V((D, 2, EL), BF16), V((2, D, EL), BF16), V((2, D, EL), BF16), V((2 * EL, D), BF16),
+        V((17, 16, D), BF16), V((2 * (L + 16), D), BF16), V((D // 8, T), BF16), V((TB, TB), BF16),
         V((2, T + 16, EL), F32), V((2, T, EL), BF16), V((2, L, T), BF16), V((2, L, T), BF16), V((2, T, L), BF16),
         V((2, T, EL), F32), V((2, T, EL), F32),
         V((2, NC * H, L), F32), V((NC, L, L), F32), V((T, L), F32), V((2, NC, H, L), F32),
@@ -570,15 +599,15 @@
         V((NR, XM, TB), BF16), V((NR, XM, TB), BF16),
         V((NR, 2, YH, TB), BF16), V((NR, 2, YH, TB), BF16), V((NR, 2, YH, TB), BF16), V((NR, 2, YH, TB), BF16),
         V((NR, 2, YM, TB), BF16), V((NR, 2, YM, TB), BF16),
-        dma((NB,)), dma((NB,)), dma, dma, dma((7,)), dma((8,)), dma((2,)), dma((2,)), dma((2,)), dma((2,)), dma, dma, dma((7,)), dma((7,)),
+        dma((NB,)), dma((NB,)), dma, dma, dma((7,)), dma((8,)), dma((2,)), dma((2,)), dma((2,)), dma((2,)), dma((2,)), dma((2,)), dma((7,)), dma((7,)),
         dma, dma, dma((NB, 7)), dma((NB, 7)),
-        dma((NR,)), dma((NR,)), dma((NR,)), dma((NR,)), dma((NR, 6)), dma((NR, 6)), dma((NR, 6)), dma((NR, 6)),
+        dma((NR,)), dma((NR,)), dma((NR,)), dma((NR,)), dma((NR,)), dma((NR, 6)), dma((NR, 6)), dma((NR, 6)), dma((NR, 6)),
     ]
     return pl.pallas_call(
         kernel,
-        out_shape=jax.ShapeDtypeStruct((D // 8, T), F32),
+        out_shape=jax.ShapeDtypeStruct((D // 8, T), BF16),
         in_specs=[hbm, vm, vm, hbm, hbm, vm, vm, vm, vm, hbm, sm, sm, sm],
-        out_specs=vm,
+        out_specs=hbm,
         scratch_shapes=scratch,
         compiler_params=pltpu.CompilerParams(
             collective_id=0, has_side_effects=True, vmem_limit_bytes=60 * 1024 * 1024
@@ -588,7 +617,7 @@
         hidden, ids.reshape(1, T), table, proj_weight, bc_weight.T.reshape(2, 16, D), dt_weight.T,
         conv_weight, conv_bias.reshape(1, EL), norm_gain.reshape(1, EL), out_weight,
         dt_bias, decay, skip,
-    ).astype(BF16)
+    )
 
 
 def solution(mesh):

time: 88.1 us -> 82.7 us (0.939)
  Pallas kernels: 85.8 us -> 80.6 us
  other arithmetic: 2.1 us -> 0 us
  local copies, waits for them, and re-layouts: 0 us -> 1.87 us
    pallas_call x1, Pallas kernels: 85.8 us -> 80.6 us  [per_device(): pl.pallas_call(kernel, out_shape=jax.ShapeDtypeStruct((D // 8, T), BF16),...]
    convert_element_type x1 -> x0, other arithmetic: 2.1 us -> none  [per_device(): return pl.pallas_call(kernel, out_shape=jax.ShapeDtypeStruct((D // 8, T),...]
    unnamed x0 -> x1, local copies, waits for them, and re-layouts: none -> 1.87 us
where the time goes in v5:
time: 82.7 us; the launch traced here: 82.5 us
  Pallas kernels  80.6 us (97%)
  local copies, waits for them, and re-layouts  1.87 us (2%)
    pallas_call x1, Pallas kernels, per_device(): pl.pallas_call(kernel, out_shape=jax.ShapeDtypeStruct((D // 8, T), BF16),...  80.6 us
    unnamed x1, local copies, waits for them, and re-layouts  1.87 us

profile of v5, /device:TPU:0, one launch (start us, length us, event | category | flops | bytes accessed | tf_op | source)
XLA Modules:
  0.0 82.5 jit_solution(15567431195964109445)
XLA Ops:
  0.0 80.6 %shard_map.127 = bf16[256,1024]{1,0:T(8,128)(2,1)} custom-call(bf16[1024,2048]{1,0:T(8,128)(2,1)} %hid_hbm.1, s32[1,1024]{1,0:T(1,128)} %bitcast.9, bf16[5,2048]{1,0:T(8,128)(2,1)} %table_ref.1, bf16[2048,2,512]{2,1,0:T(2,128)(2,1)} %w_hbm.1, bf16[2,16,2048]{2,1,0:T(8,128)(2,1)} %bitcast.7, bf16[8,2048]{1,0:T(8,128)(2,1)} %bitcast.8, f32[4,512]{1,0:T(4,128)} %cw_ref.1, ...), custom_call_target="tpu_custom_call" | custom-call | flops 20000000000 | bytes 16000000 | tf_op jit(solution)/shard_map/pallas_call | solution.py:606
  80.7 1.9 %copy.15 = bf16[256,1024]{1,0:T(8,128)(2,1)} copy(bf16[256,1024]{1,0:T(8,128)(2,1)} %shard_map.127) | data formatting | bytes 1048576

commit v6 on v5

--- a/solution.py
+++ b/solution.py
@@ -10,7 +10,7 @@
 TB = 256
 BLOCKS = (
     (0, 256, 112, 48, 80), (256, 256, 112, 48, 80), (512, 256, 112, 48, 80),
-    (768, 128, 64, 32, 32), (896, 128, 64, 32, 32),
+    (768, 128, 64, 32, 32), (896, 128, 64, 64, 64),
 )
 NR = len(BLOCKS)
 XM, XH, YM, YH = 112, 64, 144, 80
@@ -45,13 +45,13 @@
 
 
 def kernel(
-    hid_hbm, ids_ref, table_ref, w_hbm, bcw_hbm, dtw_ref, cw_ref, cb_ref, gain_ref, wo_hbm,
+    hid_hbm, ids_ref, table_ref, w_hbm, bcw_ref, dtw_ref, cw_ref, cb_ref, gain_ref, wo_hbm,
     dtb_ref, decay_ref, skip_ref,
     out_ref,
     u, wraw, wx, wg, wall, bcw, lhs, ob, flip, xin, xc, bt, ct, cm, gate, ybuf, dtraw, rowsbuf, cols, arow, sch, enter,
     halo_out, halo_in, st_out, st_in, ch_out, ch_in, fin_out, fin_in,
     sq, nrm, part, rx, qbuf, abuf, rx2, xa, xb, xaa, xba, xprev, xnext, ya, yb, yaa, yba, yprev, ynext,
-    hsem, wsem, wosem, bsem, bgs, bgr, bcs, bcr, hs, hr, sts, stsr, chs, chr_, fis, fir, sqs, sqr,
+    hsem, wsem, wosem, bgs, bgr, bcs, bcr, hs, hr, sts, stsr, chs, chr_, fis, fir, sqs, sqr,
     rxs, rxr, rx2s, rx2r, osem, xss, xsr, yss, ysr,
 ):
     T, D = u.shape
@@ -71,6 +71,16 @@
             device_id_type=MESH,
         )
 
+    mate = c + 1 - 2 * core
+    other = (c + 16 + 2 * core - 1) % 16
+    chip = c // 2
+    barrier = pltpu.get_barrier_semaphore()
+    peers = [(mate, s), (other, s)]
+    peers += [((c + 2 * k) % 16, s) for k in range(1, 8)]
+    peers += [(c, (s + k) % 8) for k in range(1, 8)]
+    for pc, ps in peers:
+        pl.semaphore_signal(barrier, inc=1, device_id={"ctx": pc, "shard": ps}, device_id_type=MESH)
+
     WR = D // NB
     hcopies = [
         pltpu.make_async_copy(hid_hbm.at[pl.ds(b * TB, TB)], u.at[pl.ds(b * TB, TB)], hsem.at[b])
@@ -81,26 +91,17 @@
         for b in range(NB)
     ]
     woc = pltpu.make_async_copy(wo_hbm, wall.at[pl.ds(0, EL)], wosem)
-    bown = pltpu.make_async_copy(bcw_hbm.at[core], bcw.at[core * 8 + s], bsem)
     for b in range(NB):
         hcopies[b].start()
     for b in range(NB):
         wcopies[b].start()
-    bown.start()
-
-    mate = c + 1 - 2 * core
-    other = (c + 16 + 2 * core - 1) % 16
-    chip = c // 2
-    barrier = pltpu.get_barrier_semaphore()
-    peers = [(mate, s), (other, s)]
-    peers += [((c + 2 * k) % 16, s) for k in range(1, 8)]
-    peers += [(c, (s + k) % 8) for k in range(1, 8)]
-    for pc, ps in peers:
-        pl.semaphore_signal(barrier, inc=1, device_id={"ctx": pc, "shard": ps}, device_id_type=MESH)
+
     pl.semaphore_wait(barrier, len(peers))
 
+    bcw[pl.ds(core * 8 + s, 1)] = bcw_ref[pl.ds(core, 1)]
+
     def gather(k):
-        return remote(bcw_hbm.at[core], bcw.at[core * 8 + s], bgs.at[k - 1], bgr.at[s], shard=(s + k) % 8)
+        return remote(bcw_ref.at[core], bcw.at[core * 8 + s], bgs.at[k - 1], bgr.at[s], shard=(s + k) % 8)
 
     for k in range(1, 8):
         gather(k).start()
@@ -151,13 +152,12 @@
         at = pl.ds(core * 8 + 4 * m, 4)
         return remote(bcw.at[at], bcw.at[at], bcs.at[m], bcr.at[m], ctx=mate)
 
-    bown.wait()
     for m in range(2):
         for src in range(4 * m, 4 * m + 4):
             @pl.when(s != src)
             def _():
                 remote(
-                    bcw_hbm.at[core], bcw.at[core * 8 + src], bgs.at[0], bgr.at[src], shard=(s + 1) % 8
+                    bcw_ref.at[core], bcw.at[core * 8 + src], bgs.at[0], bgr.at[src], shard=(s + 1) % 8
                 ).wait_recv()
         swap(m).start()
     for k in range(1, 8):
@@ -184,6 +184,12 @@
         for i in range(2):
             gate[i, rows, :] = silu(dot(u[rows, :], wg[i]))
 
+    hcf.wait()
+    hcr.wait()
+    xin[0, 0:8, :] = jnp.where(c > 0, halo_in[0, 8:16, :].astype(F32), 0.0)
+    xin[1, T + 8:T + 16, :] = jnp.where(c < 15, halo_in[1, 0:8, :].astype(F32), 0.0)
+    convolve(0, 0)
+    convolve(1, NC - 1)
     swap(0).wait()
 
     wb = jnp.concatenate([bcw[0:4], bcw[8:12], bcw[16:17]], 0).reshape(L + 16, D)
@@ -240,13 +246,7 @@
     for k in range(NC):
         cols[k * L:(k + 1) * L, :] = rowsbuf[k].T
 
-    hcf.wait()
-    hcr.wait()
-    xin[0, 0:8, :] = jnp.where(c > 0, halo_in[0, 8:16, :].astype(F32), 0.0)
-    xin[1, T + 8:T + 16, :] = jnp.where(c < 15, halo_in[1, 0:8, :].astype(F32), 0.0)
-
     def chunk_states(i):
-        convolve(i, 0 if i == 0 else NC - 1)
         for k in range(NC):
             rows = slice(k * L, (k + 1) * L)
             wexp = dot(cols[rows, :].astype(BF16), spreads[2 * i])
@@ -426,9 +426,24 @@
         n = BLOCKS[j][1] - BLOCKS[j][2]
         return remote(abuf.at[j, pl.ds(0, n)], rx2.at[j, pl.ds(0, n)], rx2s.at[j], rx2r.at[j], shard=xs)
 
+    def straight(j):
+        return BLOCKS[j][2] == BLOCKS[j][3]
+
+    def first_steps(j):
+        return range(3) if straight(j) else range(4)
+
+    def final_steps(j):
+        return range(3) if straight(j) else range(2, 6)
+
     def ring_y(j, step):
         n, xr, h0 = BLOCKS[j][1], BLOCKS[j][2], BLOCKS[j][4]
         h1 = n - xr - h0
+        if straight(j):
+            to, buf = [(up, yprev), (down, ynext), (across, ya)][step]
+            return remote(
+                part.at[j, :, to, pl.ds(xr, h0), :], buf.at[j, :, pl.ds(0, h0), :],
+                yss.at[j, step], ysr.at[j, step], shard=to * 2 + xl,
+            )
         lo, hi = pl.ds(0, h0), pl.ds(h0, h1)
         plo, phi = pl.ds(xr, h0), pl.ds(xr + h0, h1)
         src, dst, to = [
@@ -444,6 +459,12 @@
     def ring_x(j, step):
         xr, h0 = BLOCKS[j][2], BLOCKS[j][3]
         h1 = xr - h0
+        if straight(j):
+            to, buf = [(up, xprev), (down, xnext), (across, xa)][step]
+            return remote(
+                qbuf.at[j, to, pl.ds(0, xr), :], buf.at[j, pl.ds(0, xr), :],
+                xss.at[j, step], xsr.at[j, step], shard=to * 2 + xl,
+            )
         lo, hi = pl.ds(0, h0), pl.ds(h0, h1)
         src, dst, to = [
             (qbuf.at[j, across, lo, :], xa.at[j, lo, :], up),
@@ -478,18 +499,21 @@
             part[j, xx, yy, 0:n, :] = dot(nrm[rows, :], wall[:, rows_of(yy * 2 + xx, TB)]).astype(BF16)
             if p == 3:
                 cross(j).start()
-        for step in range(4):
+        for step in first_steps(j):
             ring_y(j, step).start()
 
-    def middle_block(j):
-        n, xr, h0 = BLOCKS[j][1], BLOCKS[j][2], BLOCKS[j][4]
-        h1 = n - xr - h0
+    def middle_x(j):
+        xr = BLOCKS[j][2]
         cross(j).wait()
         for yk in range(4):
             both = part[j, xl, yk, 0:xr, :].astype(F32) + rx[j, yk, 0:xr, :].astype(F32)
             qbuf[j, yk, 0:xr, :] = both.astype(BF16)
-        for step in range(4):
+        for step in first_steps(j):
             ring_x(j, step).start()
+
+    def middle_y(j):
+        n, xr, h0 = BLOCKS[j][1], BLOCKS[j][2], BLOCKS[j][4]
+        h1 = n - xr - h0
         for step in range(2):
             ring_y(j, step).wait()
         for m in range(2):
@@ -500,8 +524,8 @@
         for step in range(4, 6):
             ring_y(j, step).start()
 
-    def third_block(j):
-        n, xr, h0 = BLOCKS[j][1:4]
+    def third_x(j):
+        xr, h0 = BLOCKS[j][2:4]
         h1 = xr - h0
         for step in range(2):
             ring_x(j, step).wait()
@@ -511,26 +535,33 @@
         xba[j, 0:h1, :] = both.astype(BF16)
         for step in range(4, 6):
             ring_x(j, step).start()
-        for step in range(2, 6):
+
+    def third_y(j):
+        n, xr = BLOCKS[j][1:3]
+        for step in final_steps(j):
             ring_y(j, step).wait()
         sums_ = []
         for m in range(2):
             xx = (xl + 1 + m) % 2
             acc = part[j, xx, y, xr:n, :].astype(F32)
             acc = acc + yprev[j, xx, 0:n - xr, :].astype(F32) + ynext[j, xx, 0:n - xr, :].astype(F32)
+            if straight(j):
+                acc = acc + ya[j, xx, 0:n - xr, :].astype(F32)
             sums_.append(acc)
         abuf[j, 0:n - xr, :] = sums_[0].astype(BF16)
         cross2(j).start()
-        return sums_[1]
-
-    def last_block(j, own):
+        kept[j] = sums_[1]
+
+    def last_block(j):
         r0, n, xr = BLOCKS[j][:3]
-        for step in range(2, 6):
+        for step in final_steps(j):
             ring_x(j, step).wait()
         acc = qbuf[j, y, 0:xr, :].astype(F32)
         acc = acc + xprev[j, 0:xr, :].astype(F32) + xnext[j, 0:xr, :].astype(F32)
+        if straight(j):
+            acc = acc + xa[j, 0:xr, :].astype(F32)
         cross2(j).wait()
-        low = own + rx2[j, 0:n - xr, :].astype(F32)
+        low = kept[j] + rx2[j, 0:n - xr, :].astype(F32)
         ob[:, r0:r0 + n] = jnp.concatenate([acc, low], 0).T.astype(BF16)
         leave(j).start()
 
@@ -541,29 +572,37 @@
     kept = [None] * len(BLOCKS)
     gated_block(0)
     gated_block(1)
+    gated_block(2)
     late_block(3)
     product_block(0)
-    gated_block(2)
     product_block(1)
     gated_block(3)
-    middle_block(0)
+    middle_y(0)
     product_block(2)
-    middle_block(1)
-    kept[0] = third_block(0)
+    middle_y(1)
+    middle_x(0)
     product_block(3)
-    middle_block(2)
-    kept[1] = third_block(1)
+    middle_y(2)
     product_block(4)
-    last_block(0, kept[0])
-    middle_block(3)
-    kept[2] = third_block(2)
-    middle_block(4)
-    last_block(1, kept[1])
-    kept[3] = third_block(3)
-    kept[4] = third_block(4)
-    last_block(2, kept[2])
-    last_block(3, kept[3])
-    last_block(4, kept[4])
+    middle_x(1)
+    third_y(0)
+    third_x(0)
+    middle_y(3)
+    middle_x(2)
+    third_y(1)
+    third_x(1)
+    last_block(0)
+    middle_x(3)
+    third_y(2)
+    third_x(2)
+    middle_x(4)
+    third_y(3)
+    third_x(3)
+    third_y(4)
+    last_block(1)
+    last_block(2)
+    last_block(3)
+    last_block(4)
     for j in range(NR):
         leave(j).wait()
 
@@ -599,14 +638,14 @@
         V((NR, XM, TB), BF16), V((NR, XM, TB), BF16),
         V((NR, 2, YH, TB), BF16), V((NR, 2, YH, TB), BF16), V((NR, 2, YH, TB), BF16), V((NR, 2, YH, TB), BF16),
         V((NR, 2, YM, TB), BF16), V((NR, 2, YM, TB), BF16),
-        dma((NB,)), dma((NB,)), dma, dma, dma((7,)), dma((8,)), dma((2,)), dma((2,)), dma((2,)), dma((2,)), dma((2,)), dma((2,)), dma((7,)), dma((7,)),
+        dma((NB,)), dma((NB,)), dma, dma((7,)), dma((8,)), dma((2,)), dma((2,)), dma((2,)), dma((2,)), dma((2,)), dma((2,)), dma((7,)), dma((7,)),
         dma, dma, dma((NB, 7)), dma((NB, 7)),
         dma((NR,)), dma((NR,)), dma((NR,)), dma((NR,)), dma((NR,)), dma((NR, 6)), dma((NR, 6)), dma((NR, 6)), dma((NR, 6)),
     ]
     return pl.pallas_call(
         kernel,
         out_shape=jax.ShapeDtypeStruct((D // 8, T), BF16),
-        in_specs=[hbm, vm, vm, hbm, hbm, vm, vm, vm, vm, hbm, sm, sm, sm],
+        in_specs=[hbm, vm, vm, hbm, vm, vm, vm, vm, vm, hbm, sm, sm, sm],
         out_specs=hbm,
         scratch_shapes=scratch,
         compiler_params=pltpu.CompilerParams(

time: 82.7 us -> 82.8 us (level)
  no operation moved by 1% of the time
where the time goes in v6:
time: 82.8 us; the launch traced here: 82.7 us
  Pallas kernels  80.8 us (98%)
  local copies, waits for them, and re-layouts  1.87 us (2%)
    pallas_call x1, Pallas kernels, per_device(): pl.pallas_call(kernel, out_shape=jax.ShapeDtypeStruct((D // 8, T), BF16),...  80.8 us
    unnamed x1, local copies, waits for them, and re-layouts  1.87 us

profile of v6, /device:TPU:0, one launch (start us, length us, event | category | flops | bytes accessed | tf_op | source)
XLA Modules:
  0.0 82.7 jit_solution(2055250286583970043)
XLA Ops:
  0.0 80.8 %shard_map.127 = bf16[256,1024]{1,0:T(8,128)(2,1)} custom-call(bf16[1024,2048]{1,0:T(8,128)(2,1)} %hid_hbm.1, s32[1,1024]{1,0:T(1,128)} %bitcast.9, bf16[5,2048]{1,0:T(8,128)(2,1)} %table_ref.1, bf16[2048,2,512]{2,1,0:T(2,128)(2,1)} %w_hbm.1, bf16[2,16,2048]{2,1,0:T(8,128)(2,1)} %bitcast.7, bf16[8,2048]{1,0:T(8,128)(2,1)} %bitcast.8, f32[4,512]{1,0:T(4,128)} %cw_ref.1, ...), custom_call_target="tpu_custom_call" | custom-call | flops 20000000000 | bytes 16000000 | tf_op jit(solution)/shard_map/pallas_call | solution.py:645
  80.8 1.9 %copy.15 = bf16[256,1024]{1,0:T(8,128)(2,1)} copy(bf16[256,1024]{1,0:T(8,128)(2,1)} %shard_map.127) | data formatting | bytes 1048576

commit v7 on v5

--- a/solution.py
+++ b/solution.py
@@ -481,15 +481,18 @@
         for step in range(4):
             ring_y(j, step).start()
 
-    def middle_block(j):
-        n, xr, h0 = BLOCKS[j][1], BLOCKS[j][2], BLOCKS[j][4]
-        h1 = n - xr - h0
+    def middle_x(j):
+        xr = BLOCKS[j][2]
         cross(j).wait()
         for yk in range(4):
             both = part[j, xl, yk, 0:xr, :].astype(F32) + rx[j, yk, 0:xr, :].astype(F32)
             qbuf[j, yk, 0:xr, :] = both.astype(BF16)
         for step in range(4):
             ring_x(j, step).start()
+
+    def middle_y(j):
+        n, xr, h0 = BLOCKS[j][1], BLOCKS[j][2], BLOCKS[j][4]
+        h1 = n - xr - h0
         for step in range(2):
             ring_y(j, step).wait()
         for m in range(2):
@@ -500,8 +503,8 @@
         for step in range(4, 6):
             ring_y(j, step).start()
 
-    def third_block(j):
-        n, xr, h0 = BLOCKS[j][1:4]
+    def third_x(j):
+        xr, h0 = BLOCKS[j][2:4]
         h1 = xr - h0
         for step in range(2):
             ring_x(j, step).wait()
@@ -511,6 +514,9 @@
         xba[j, 0:h1, :] = both.astype(BF16)
         for step in range(4, 6):
             ring_x(j, step).start()
+
+    def third_y(j):
+        n, xr = BLOCKS[j][1:3]
         for step in range(2, 6):
             ring_y(j, step).wait()
         sums_ = []
@@ -521,16 +527,16 @@
             sums_.append(acc)
         abuf[j, 0:n - xr, :] = sums_[0].astype(BF16)
         cross2(j).start()
-        return sums_[1]
-
-    def last_block(j, own):
+        kept[j] = sums_[1]
+
+    def last_block(j):
         r0, n, xr = BLOCKS[j][:3]
         for step in range(2, 6):
             ring_x(j, step).wait()
         acc = qbuf[j, y, 0:xr, :].astype(F32)
         acc = acc + xprev[j, 0:xr, :].astype(F32) + xnext[j, 0:xr, :].astype(F32)
         cross2(j).wait()
-        low = own + rx2[j, 0:n - xr, :].astype(F32)
+        low = kept[j] + rx2[j, 0:n - xr, :].astype(F32)
         ob[:, r0:r0 + n] = jnp.concatenate([acc, low], 0).T.astype(BF16)
         leave(j).start()
 
@@ -545,25 +551,35 @@
     product_block(0)
     gated_block(2)
     product_block(1)
+    middle_y(0)
     gated_block(3)
-    middle_block(0)
     product_block(2)
-    middle_block(1)
-    kept[0] = third_block(0)
+    middle_y(1)
+    middle_x(0)
     product_block(3)
-    middle_block(2)
-    kept[1] = third_block(1)
+    middle_y(2)
     product_block(4)
-    last_block(0, kept[0])
-    middle_block(3)
-    kept[2] = third_block(2)
-    middle_block(4)
-    last_block(1, kept[1])
-    kept[3] = third_block(3)
-    kept[4] = third_block(4)
-    last_block(2, kept[2])
-    last_block(3, kept[3])
-    last_block(4, kept[4])
+    middle_x(1)
+    third_y(0)
+    third_x(0)
+    middle_y(3)
+    middle_x(2)
+    third_y(1)
+    third_x(1)
+    middle_y(4)
+    last_block(0)
+    middle_x(3)
+    third_y(2)
+    third_x(2)
+    middle_x(4)
+    third_y(3)
+    third_x(3)
+    last_block(1)
+    third_y(4)
+    third_x(4)
+    last_block(2)
+    last_block(3)
+    last_block(4)
     for j in range(NR):
         leave(j).wait()
 

time: 82.7 us -> 82.8 us (level)
  no operation moved by 1% of the time
where the time goes in v7:
time: 82.8 us; the launch traced here: 82.6 us
  Pallas kernels  80.7 us (97%)
  local copies, waits for them, and re-layouts  1.87 us (2%)
    pallas_call x1, Pallas kernels, per_device(): pl.pallas_call(kernel, out_shape=jax.ShapeDtypeStruct((D // 8, T), BF16),...  80.7 us
    unnamed x1, local copies, waits for them, and re-layouts  1.87 us

profile of v7, /device:TPU:0, one launch (start us, length us, event | category | flops | bytes accessed | tf_op | source)
XLA Modules:
  0.0 82.6 jit_solution(6299903430915263241)
XLA Ops:
  0.0 80.7 %shard_map.127 = bf16[256,1024]{1,0:T(8,128)(2,1)} custom-call(bf16[1024,2048]{1,0:T(8,128)(2,1)} %hid_hbm.1, s32[1,1024]{1,0:T(1,128)} %bitcast.9, bf16[5,2048]{1,0:T(8,128)(2,1)} %table_ref.1, bf16[2048,2,512]{2,1,0:T(2,128)(2,1)} %w_hbm.1, bf16[2,16,2048]{2,1,0:T(8,128)(2,1)} %bitcast.7, bf16[8,2048]{1,0:T(8,128)(2,1)} %bitcast.8, f32[4,512]{1,0:T(4,128)} %cw_ref.1, ...), custom_call_target="tpu_custom_call" | custom-call | flops 20000000000 | bytes 16000000 | tf_op jit(solution)/shard_map/pallas_call | solution.py:622
  80.7 1.9 %copy.15 = bf16[256,1024]{1,0:T(8,128)(2,1)} copy(bf16[256,1024]{1,0:T(8,128)(2,1)} %shard_map.127) | data formatting | bytes 1048576
